TPU v7x, 256 devices: a whole 4x4x8 slice. The times are simulated.
256 devices in a mesh: dp: 32 (over z, y_lo, core), replica: 8 (over y_hi, x).
Axes of the slice: x: 4, y: 4 (y_hi: 2, y_lo: 2; y = y_hi * 2 + y_lo), z: 8, core: 2. Of those that a mesh axis runs over, the one named last changes fastest.
Arguments:
- first_view: float32 [8192, 4096], P('dp'), may hold values from -266 to 266
- second_view: float32 [8192, 4096], P('dp'), may hold values from -266 to 266
Outputs:
- grad_first: float32 [8192, 4096], P('dp', 'replica')
- grad_second: float32 [8192, 4096], P('dp', 'replica')
All inputs are finite; a program needn't handle non-finite values.
Results may differ from a plain program's by a relative error of at most 0.015.
Values may be sent and summed in bfloat16 or wider, within the bound.
A program may use at most 128 MiB of HBM per device.

v0:
```python
import jax
import jax.numpy as jnp
from jax import lax
from jax.sharding import PartitionSpec as P

LAMBDA = 0.0051
EPS = 1e-05


def body(first_view, second_view):
    rows, width = first_view.shape
    n_dp = lax.axis_size("dp")
    n_rep = lax.axis_size("replica")
    batch = rows * n_dp
    first_width = width // n_dp
    second_width = width // n_rep
    dp_index = lax.axis_index("dp")
    rep_index = lax.axis_index("replica")
    second_offset = rep_index * second_width
    first_offset = dp_index * first_width
    totals = lax.psum((jnp.sum(first_view, 0), jnp.sum(second_view, 0)), "dp")
    dev_first = first_view - totals[0] / batch
    dev_second = second_view - totals[1] / batch
    squares = lax.psum(
        (jnp.sum(dev_first * dev_first, 0), jnp.sum(dev_second * dev_second, 0)), "dp"
    )
    var_first = squares[0] / batch
    var_second = squares[1] / batch
    rstd_first = lax.rsqrt(var_first + EPS)
    rstd_second = lax.rsqrt(var_second + EPS)
    norm_first = dev_first * rstd_first
    norm_second = dev_second * rstd_second
    sent_first = norm_first.astype(jnp.bfloat16)
    sent_second = norm_second.astype(jnp.bfloat16)
    cols_first = lax.all_to_all(sent_first, "dp", split_axis=1, concat_axis=0, tiled=True)
    own_second = lax.dynamic_slice_in_dim(sent_second, second_offset, second_width, 1)
    gathered = lax.all_gather(own_second, "dp", axis=0, tiled=True)
    total = lax.dot_general(
        cols_first, gathered, (((0,), (0,)), ((), ())), preferred_element_type=jnp.float32
    )
    corr = total / batch
    row_ids = first_offset + lax.broadcasted_iota(jnp.int32, (first_width, second_width), 0)
    col_ids = second_offset + lax.broadcasted_iota(jnp.int32, (first_width, second_width), 1)
    grad_block = jnp.where(row_ids == col_ids, -2.0 * (1.0 - corr), 2.0 * LAMBDA * corr).astype(
        jnp.bfloat16
    )
    grad_norm_second = jnp.dot(
        sent_first,
        lax.all_gather(grad_block, "dp", axis=0, tiled=True),
        preferred_element_type=jnp.float32,
    )
    first_full = lax.dot_general(
        gathered, grad_block, (((1,), (1,)), ((), ())), preferred_element_type=jnp.float32
    )
    first_rows = lax.all_to_all(
        first_full.astype(jnp.bfloat16), "dp", split_axis=0, concat_axis=1, tiled=True
    ).astype(first_full.dtype)
    grad_norm_first = lax.psum_scatter(
        first_rows.astype(jnp.bfloat16), "replica", scatter_dimension=1, tiled=True
    ).astype(jnp.float32)
    norm_first_block = lax.dynamic_slice_in_dim(norm_first, second_offset, second_width, 1)
    norm_second_block = lax.dynamic_slice_in_dim(norm_second, second_offset, second_width, 1)
    rstd_first_block = lax.dynamic_slice_in_dim(rstd_first, second_offset, second_width, 0)
    rstd_second_block = lax.dynamic_slice_in_dim(rstd_second, second_offset, second_width, 0)
    block_stats = lax.psum(
        (
            jnp.sum(grad_norm_first, 0),
            jnp.sum(grad_norm_first * norm_first_block, 0),
            jnp.sum(grad_norm_second, 0),
            jnp.sum(grad_norm_second * norm_second_block, 0),
        ),
        "dp",
    )
    grad_first = rstd_first_block * (
        grad_norm_first - block_stats[0] / batch - norm_first_block * (block_stats[1] / batch)
    )
    grad_second = rstd_second_block * (
        grad_norm_second - block_stats[2] / batch - norm_second_block * (block_stats[3] / batch)
    )
    return (grad_first, grad_second)


def solution(mesh):
    in_specs = (P("dp", None), P("dp", None))
    out_specs = (P("dp", "replica"), P("dp", "replica"))
    return jax.shard_map(body, mesh=mesh, in_specs=in_specs, out_specs=out_specs, check_vma=False)
```

profile of v0, /device:TPU:1, one launch (start us, length us, event | category | flops | bytes accessed | tf_op | source)
XLA Modules:
  0.0 597.8 jit_solution(5746322483764082811)
XLA Ops:
  7.2 0.0 all-gather.3.cloned.1.call-start
  7.2 5.6 copy.6
  12.8 2.4 reduce_sum.72
  15.2 2.4 reduce_sum.74
  17.6 107.7 %all-reduce.2 = (f32[4096]{0:T(1024)S(1)}, f32[4096]{0:T(1024)S(1)}) all-reduce(f32[4096]{0:T(1024)S(1)} %reduce_sum.74, f32[4096]{0:T(1024)S(1)} %reduce_sum.72), channel_id=1, replica_groups=mesh['dp'=32,'replica'=8] {'dp'}, use_global_device_ids=true, to_apply=%region_5.0 | all-reduce | flops 8192 | bytes 65536 | tf_op jit(solution)/shard_map/psum | solution.py:21
  125.4 0.0 copy-start
  125.4 2.8 multiply_reduce_fusion
  128.2 0.6 copy-done
  128.8 1.3 multiply_reduce_fusion.1
  130.1 104.4 %all-reduce.1 = (f32[4096]{0:T(1024)S(1)}, f32[4096]{0:T(1024)S(1)}) all-reduce(f32[4096]{0:T(1024)S(1)} %multiply_reduce_fusion, f32[4096]{0:T(1024)S(1)} %multiply_reduce_fusion.1), channel_id=1, replica_groups=mesh['dp'=32,'replica'=8] {'dp'}, use_global_device_ids=true, to_apply=%region_7.0 | all-reduce | flops 8192 | bytes 65536 | tf_op jit(solution)/shard_map/psum | solution.py:24
  234.5 4.8 subtract_multiply_fusion
  239.3 1.8 dynamic-slice_convert_fusion
  241.1 0.0 all-gather.3.cloned.1.call-update
  241.2 4.8 fusion.15
  246.0 8.1 %all-to-all-start = ((bf16[256,32,128]{0,2,1:T(8,128)(2,1)}), bf16[256,32,128]{0,2,1:T(8,128)(2,1)S(1)}, u32[]{:S(2)}, u32[]{:S(2)}) async-start(bf16[256,32,128]{0,2,1:T(8,128)(2,1)} %bitcast), calls=%async_computation | async-start | bytes 4194304 | tf_op jit(solution)/shard_map/all_to_all | solution.py:35
  254.1 0.0 all-gather.5.cloned.1.call-start
  254.2 72.7 %all-to-all-done = bf16[256,32,128]{0,2,1:T(8,128)(2,1)S(1)} async-done(((bf16[256,32,128]{0,2,1:T(8,128)(2,1)}), bf16[256,32,128]{0,2,1:T(8,128)(2,1)S(1)}, u32[]{:S(2)}, u32[]{:S(2)}) %all-to-all-start) | async-done | bytes 2097184 | tf_op jit(solution)/shard_map/all_to_all | solution.py:35
  326.9 0.0 copy-start.1
  326.9 1.4 copy-done.1
  328.2 3.2 copy.7
  331.5 21.8 %all-gather.3.cloned.1.call-done = bf16[8192,512]{1,0:T(8,128)(2,1)} async-done(((bf16[256,512]{1,0:T(8,128)(2,1)}), bf16[8192,512]{1,0:T(8,128)(2,1)}) %all-gather.3.cloned.1.call-update) | async-done | bytes 8388624 | tf_op jit(solution)/shard_map/all_gather | solution.py:37
  353.3 5.4 select_convert_fusion
  358.6 0.0 all-gather.5.cloned.1.call-update
  358.6 0.0 reduce-scatter.2.cloned.1.call-start
  358.7 5.8 convolution_convert_fusion
  364.5 72.9 %all_to_all.38 = bf16[32,256,128]{2,1,0:T(8,128)(2,1)S(1)} all-to-all(bf16[32,256,128]{2,1,0:T(8,128)(2,1)S(1)} %bitcast.12), channel_id=1, replica_groups=mesh['dp'=32,'replica'=8] {'dp'}, dimensions={0} | all-to-all | bytes 4194304 | tf_op jit(solution)/shard_map/all_to_all | solution.py:55
  437.4 2.9 copy.8
  440.4 0.0 reduce-scatter.2.cloned.1.call-update
  440.4 0.1 dynamic_slice.18
  440.5 0.1 dynamic_slice.15
  440.5 6.9 %all-gather.5.cloned.1.call-done = bf16[4096,512]{1,0:T(8,128)(2,1)} async-done(((bf16[128,512]{1,0:T(8,128)(2,1)}), bf16[4096,512]{1,0:T(8,128)(2,1)}) %all-gather.5.cloned.1.call-update) | async-done | bytes 4194320 | tf_op jit(solution)/shard_map/all_gather | solution.py:49
  447.5 4.2 fusion.14
  451.6 78.4 %reduce-scatter.2.cloned.1.call-done = bf16[256,512]{0,1:T(8,128)(2,1)} async-done(((bf16[256,4096]{0,1:T(8,128)(2,1)}), bf16[256,512]{0,1:T(8,128)(2,1)}) %reduce-scatter.2.cloned.1.call-update) | async-done | bytes 262160 | tf_op jit(solution)/shard_map/reduce_scatter | solution.py:58
  530.1 1.3 convert_reduce_fusion
  531.4 55.5 %all-reduce = (f32[512]{0:T(512)S(1)}, f32[512]{0:T(512)S(1)}, f32[512]{0:T(512)S(1)}, f32[512]{0:T(512)S(1)}) all-reduce(f32[512]{0:T(512)S(1)} %get-tuple-element.7, f32[512]{0:T(512)S(1)} %get-tuple-element.6, f32[512]{0:T(512)S(1)} %get-tuple-element.5, f32[512]{0:T(512)S(1)} %get-tuple-element.4), channel_id=1, replica_groups=mesh['dp'=32,'replica'=8] {'dp'}, use_global_device_ids=true, to_apply=%region_12.13 | all-reduce | flops 2048 | bytes 16384 | tf_op jit(solution)/shard_map/psum | solution.py:65
  586.9 1.4 fusion.1
  588.4 1.0 copy.9
  589.4 1.9 subtract_multiply_fusion.2
  (9 shorter events, 0.0 us)
Async XLA Ops:
  7.2 346.1 %all-gather.3.cloned.1.call-start = ((), (), s32[]{:S(2)}) async-start(), calls=%async_computation.3 | async-start | bytes 8650752 | tf_op jit(solution)/shard_map/all_gather | solution.py:37
  125.4 3.4 copy-start
  246.0 80.9 %all-to-all-start = ((bf16[256,32,128]{0,2,1:T(8,128)(2,1)}), bf16[256,32,128]{0,2,1:T(8,128)(2,1)S(1)}, u32[]{:S(2)}, u32[]{:S(2)}) async-start(bf16[256,32,128]{0,2,1:T(8,128)(2,1)} %bitcast), calls=%async_computation | async-start | bytes 4194304 | tf_op jit(solution)/shard_map/all_to_all | solution.py:35
  254.1 193.4 %all-gather.5.cloned.1.call-start = ((), (), s32[]{:S(2)}) async-start(), calls=%async_computation.5 | async-start | bytes 4325376 | tf_op jit(solution)/shard_map/all_gather | solution.py:49
  326.9 1.4 copy-start.1
  358.6 171.4 %reduce-scatter.2.cloned.1.call-start = ((), (), s32[]{:S(2)}) async-start(), calls=%async_computation.4 | async-start | bytes 2359296 | tf_op jit(solution)/shard_map/reduce_scatter | solution.py:58
Sparse Core Ops, SparseCore 0:
  241.3 111.9 all-gather.2
  358.8 88.6 all-gather.4
  451.5 78.4 reduce-scatter.1
where the time goes:
time: 599 us; the launch traced here: 598 us
  blocking collectives  341 us (57%)
  waiting for transfers between devices  180 us (30%)
  other arithmetic  23.2 us (4%)
  local copies, waits for them, and re-layouts  16.7 us (3%)
  matrix products  15.3 us (3%)
  between operations  13.9 us (2%)
  starting transfers between devices  8.22 us (1%)
    psum x1, blocking collectives, body(): totals = lax.psum((jnp.sum(first_view, 0), jnp.sum(second_view, 0)), 'dp')  108 us
    psum x1, blocking collectives, body(): lax.psum((jnp.sum(dev_first * dev_first, 0), jnp.sum(dev_second * dev_sec...  104 us
    reduce_scatter x1, waiting for transfers between devices, body(): lax.psum_scatter(first_rows.astype(jnp.bfloat16), 'replica', scatter_dime...  78.4 us
    all_to_all x1, blocking collectives, body(): lax.all_to_all(first_full.astype(jnp.bfloat16), 'dp', split_axis=0, conca...  72.9 us
    all_to_all x1, waiting for transfers between devices, body(): lax.all_to_all(sent_first, 'dp', split_axis=1, concat_axis=0, tiled=True)  72.7 us
    psum x1, blocking collectives, body(): lax.psum((jnp.sum(grad_norm_first, 0), jnp.sum(grad_norm_first * norm_fir...  55.5 us
    all_gather x1, waiting for transfers between devices, body(): gathered = lax.all_gather(own_second, 'dp', axis=0, tiled=True)  21.8 us
  transfers between devices with their start and end apart: 4, of which 4 were waited for; matrix products, arithmetic and copies ran while one was open for 4% of the time, Pallas kernels for 0%

commit v1 on v0

v1 whole, which is shorter than its diff:
```python
import jax
import jax.numpy as jnp
from jax import lax
from jax.experimental import pallas as pl
from jax.experimental.pallas import tpu as pltpu
from jax.sharding import PartitionSpec as P

LAMBDA = 0.0051
EPS = 1e-05
MESH = pl.DeviceIdType.MESH
F32 = jnp.float32
BF16 = jnp.bfloat16
BATCH = 8192

OWN = (2, 1, 8, 9, 3, 7, 10, 11)
STAT_SIB = (1, 2, 0, 4)
STAT_NON = (1, 2, 5, 6)
KB = (2, 3, 6, 7)
AB = (0, 1, 4, 5)

M_Y = 0
M_ST1 = 11
M_ST2 = 16
M_C = 23
M_ZR = 31
M_ZG = 47
M_GD = 63
M_P1O = 79
M_P1S = 81
M_P1N = 83
M_P2O = 85
M_P2R = 87
M_P2L = 89
M_X = 91
M_ALL = 92

HIGH = lax.Precision.HIGHEST


def nt(a, b, precision=None):
    return lax.dot_general(
        a, b, (((1,), (1,)), ((), ())), preferred_element_type=F32, precision=precision
    )


def tn(a, b, precision=None):
    return lax.dot_general(
        a, b, (((0,), (0,)), ((), ())), preferred_element_type=F32, precision=precision
    )


def nn(a, b):
    return lax.dot_general(a, b, (((1,), (0,)), ((), ())), preferred_element_type=F32)


def ab(a):
    return a + 2 * lax.div(a, 2)


def kb(k):
    return k + 2 + 2 * lax.div(k, 2)


def kernel(
    first, second, out1, out2,
    raw, cen, oth, xt, stat, smsg, st1, st2m, st2, fin, scl, fix, nrm, cown, csend, crecv, zs, zr, g,
    acc1, acc2, rsq, csq, rowsq, colsq,
    p1, p1in, p1relay, p2, p2in, p2relay, xs, xr, ob1, ob2, ss, rs, ls, os_,
):
    dp = lax.axis_index("dp")
    rep = lax.axis_index("replica")
    c = lax.rem(dp, 2)
    ylo = lax.rem(lax.div(dp, 2), 2)
    z = lax.div(dp, 4)
    yhi = lax.div(rep, 4)
    x = lax.rem(rep, 4)

    def dev(x_, yhi_, ylo_, z_, c_):
        return (z_ * 4 + ylo_ * 2 + c_, yhi_ * 4 + x_)

    core = dev(x, yhi, ylo, z, 1 - c)
    sib = dev(x, yhi, 1 - ylo, z, c)
    sibc = dev(x, yhi, 1 - ylo, z, 1 - c)
    non = dev(x, 1 - yhi, 1 - ylo, z, c)
    nonc = dev(x, 1 - yhi, 1 - ylo, z, 1 - c)
    right = dev(lax.rem(x + 1, 4), yhi, ylo, z, c)
    left = dev(lax.rem(x + 3, 4), yhi, ylo, z, c)
    zdev = [dev(x, yhi, ylo, lax.rem(z + q, 8), c) for q in range(8)]
    zto = (zdev[1], zdev[7])

    def load(i, ref, col):
        return pltpu.make_async_copy(
            ref.at[:, pl.ds(pl.multiple_of(col, 256), 256)], raw.at[i], ls.at[i]
        )

    pieces = [lax.rem(x + k, 4) * 512 for k in range(4)]
    base = yhi * 2048
    mine = x * 512
    lo = ylo * 256
    hi = 256 - lo
    loads = [
        load(0, second, base + pieces[0] + hi),
        load(1, first, base + mine + hi),
        load(2, first, base + mine + lo),
        load(3, first, 2048 - base + mine + lo),
        load(4, second, base + pieces[1] + hi),
        load(5, second, 2048 - base + pieces[2] + hi),
        load(6, second, 2048 - base + pieces[3] + hi),
        load(7, first, 2048 - base + mine + hi),
    ] + [load(8 + k, second, base + pieces[k] + lo) for k in range(4)]
    for cp in loads:
        cp.start()

    barrier = pltpu.get_barrier_semaphore()
    partners = [core, sib, sibc, non, nonc, right, left] + zdev[1:]
    for d in partners:
        pl.semaphore_signal(barrier, inc=1, device_id=d, device_id_type=MESH)

    def make(i, src, dst, to):
        return pltpu.make_async_remote_copy(
            src_ref=src, dst_ref=dst, send_sem=ss.at[i], recv_sem=rs.at[i], device_id=to, device_id_type=MESH
        )

    sends = []

    def send(i, src, dst, to):
        cp = make(i, src, dst, to)
        cp.start()
        sends.append(cp)
        return cp

    def local_stats(i, carry):
        pltpu.make_async_copy(first.at[:, pl.ds(0, 256)], raw.at[i], ls.at[i]).wait()
        v = raw[i]
        m = jnp.sum(v, 0, keepdims=True) * (1.0 / 256)
        dv = v - m
        r = dv.astype(BF16)
        cen[i] = r
        stat[i, 0:1, :] = m
        stat[i, 1:2, :] = jnp.sum(dv * dv, 0, keepdims=True)
        stat[i, 2:3, :] = jnp.sum(r.astype(F32), 0, keepdims=True)
        stat[i, 3:4, :] = jnp.zeros_like(m)
        return carry

    top, low = pl.ds(0, 128), pl.ds(128, 128)
    lax.fori_loop(0, 1, local_stats, 0)
    pl.semaphore_wait(barrier, len(partners))
    yk0 = send(M_Y + 0, cen.at[0], oth.at[2], sib)
    lax.fori_loop(1, 4, local_stats, 0)
    xin0 = [
        send(M_Y + 1, cen.at[1], oth.at[0], sib),
        send(M_Y + 2, cen.at[1], oth.at[4], non),
    ]
    xin1 = [
        send(M_Y + 3, cen.at[2, top], oth.at[1, top], sib),
        send(M_Y + 4, cen.at[3, low], oth.at[1, low], non),
    ]
    xin2 = [send(M_Y + 5, cen.at[2], oth.at[5], non)]
    lax.fori_loop(4, 12, local_stats, 0)

    def comoment(i, j):
        return jnp.sum((raw[i] - stat[i, 0:1, :]) * (raw[j] - stat[j, 0:1, :]), 0, keepdims=True)

    for n in range(4):
        smsg[0, n] = stat[STAT_SIB[n]]
        smsg[1, n] = stat[STAT_NON[n]]
    for b in range(8):
        st1[0, b] = stat[OWN[b]]
    smsg[0, 0, 3:4, :] = comoment(1, 0)
    st1[0, 0, 3:4, :] = comoment(2, 8)
    st_in = [
        send(M_ST1 + 0, smsg.at[0], st1.at[2, pl.ds(0, 4)], sib),
        send(M_ST1 + 1, smsg.at[1], st1.at[2, pl.ds(4, 4)], non),
        send(M_ST1 + 2, smsg.at[0], st1.at[3, pl.ds(0, 4)], sibc),
        send(M_ST1 + 3, smsg.at[1], st1.at[3, pl.ds(4, 4)], nonc),
        send(M_ST1 + 4, st1.at[0], st1.at[1], core),
    ]
    yk0.wait_recv()
    yk1 = send(M_Y + 6, oth.at[2], oth.at[3], left)
    yk3 = send(M_Y + 7, oth.at[2], oth.at[7], right)
    for a in range(4):
        xt[0, a] = cen[OWN[AB[a]]].T
    for cp in st_in:
        cp.wait_recv()
    yk1.wait_recv()
    yk2 = [send(M_Y + 8, oth.at[3, top], oth.at[6, top], left)]
    yk3.wait_recv()
    yk2.append(send(M_Y + 9, oth.at[7, low], oth.at[6, low], right))

    def merge(rows_of, slots, count):
        devs = []
        res = []
        for b in range(8):
            rows = [rows_of(s, b) for s in range(slots)]
            total = sum(rows[1:], rows[0])
            m = total[0:1] * (1.0 / slots)
            dv = [r[0:1] - m for r in rows]
            m2 = total[1:2] + count * sum([d * d for d in dv[1:]], dv[0] * dv[0])
            devs.append(dv)
            res.append([m, m2, total[2:3], total[3:4]])
        cross = sum([p * q for p, q in zip(devs[0][1:], devs[2][1:])], devs[0][0] * devs[2][0])
        res[0][3] = res[0][3] + count * cross
        return res

    for b, r in enumerate(merge(lambda s, b: st1[s, b], 4, 256.0)):
        for n in range(4):
            st2m[0, b, n : n + 1, :] = r[n]
    for q in range(8):
        zq = lax.rem(z + q, 8)
        fa = ab(2 * c + lax.div(zq, 4))
        fk = kb(lax.rem(zq, 4))
        if q:
            for b in range(8):
                st2m[q, b] = st2m[0, b]
        for s in range(4):
            st2m[q, 8, s : s + 1, :] = st1[s, fa, 0:1, :]
            st2m[q, 9, s : s + 1, :] = st1[s, fk, 0:1, :]
    st2_in = [send(M_ST2 + q - 1, st2m.at[q], st2.at[q - 1], zdev[q]) for q in range(1, 8)]

    for cps, a in ((xin0, (0, 2)), (xin1, (1,)), (xin2, (3,))):
        for cp in cps:
            cp.wait_recv()
        for n in a:
            xt[1, n] = oth[AB[n]].T
    for cp in yk2:
        cp.wait_recv()

    def corr(s, carry):
        r = jnp.where(lax.rem(s, 2) == 1, 4 - lax.div(s + 1, 2), 4 + lax.div(s, 2))
        d = lax.rem(z + r, 8)
        i = lax.div(d, 4)
        k = lax.rem(d, 4)
        y0 = cen[8 + k]
        y1 = oth[kb(k)]
        a = 2 * (1 - c) + i
        csend[s] = (nn(xt[0, a], y0) + nn(xt[1, a], y1)).astype(BF16)
        make(M_C + s, csend.at[s], crecv.at[s], core).start()
        a = 2 * c + i
        cown[s] = nn(xt[0, a], y0) + nn(xt[1, a], y1)
        return carry

    def c_recv(s):
        make(M_C + s, csend.at[s], crecv.at[s], core).wait_recv()

    def zslot(d, t, u):
        return d * 8 + (t - 1) * 2 + u

    z_in = {}

    def chain(t):
        dist = 5 - t
        slot = (8 - 2 * dist - 1, 8 - 2 * dist) if dist < 4 else (0, 0)
        for d in range(2):
            if t > 1 or d == 0:
                c_recv(slot[d])
        for u in range(2):
            for d in range(2):
                if t == 1 and u != d:
                    continue
                n = slot[d]
                v = cown[n, 128 * u : 128 * u + 128] + crecv[n, 128 * u : 128 * u + 128].astype(F32)
                if (d, t - 1, u) in z_in:
                    z_in[(d, t - 1, u)].wait_recv()
                    v = v + zr[zslot(d, t - 1, u)].astype(F32)
                i = zslot(d, t, u)
                zs[i] = v.astype(BF16)
                z_in[(d, t, u)] = send(M_ZR + i, zs.at[i], zr.at[i], zto[d])

    lax.fori_loop(0, 3, corr, 0)
    chain(1)
    lax.fori_loop(3, 8, corr, 0)
    chain(2)

    for cp in st2_in:
        cp.wait_recv()
    whole = merge(lambda s, b: st2m[0, b] if s == 0 else st2[s - 1, b], 8, 1024.0)
    rstds = []
    for b, r in enumerate(whole):
        rstd = lax.rsqrt(r[1] * (1.0 / BATCH) + EPS)
        fin[b, 0:1, :] = r[0] + r[2] * (1.0 / BATCH)
        fin[b, 1:2, :] = rstd
        fin[b, 2:3, :] = r[0]
        fin[b, 3:4, :] = jnp.zeros_like(rstd)
        rstds.append(rstd)
    cii = whole[0][3] * rstds[0] * rstds[2] * (1.0 / BATCH)
    fin[8, 0:1, :] = cii
    fin[8, 1:2, :] = (-2.0 * (1.0 - cii)).astype(BF16).astype(F32)

    def norm(b, carry):
        for src, slot, o in ((None, 0, 0), (oth, 2, 1)):
            shift = st1[slot, b, 0:1, :] - fin[b, 0:1, :]
            scale = fin[b, 1:2, :]
            for h in range(2):
                rows = slice(128 * h, 128 * h + 128)
                v = own_block(b, h) if o == 0 else oth[b, rows]
                nrm[b, o * 256 + 128 * h : o * 256 + 128 * h + 128, :] = (
                    (v.astype(F32) + shift) * scale
                ).astype(BF16)
        return carry

    def own_block(b, h):
        p = lax.div(b, 4)
        q = lax.rem(b, 4)
        view1 = jnp.where(p == 0, 2 - q, 3 + 4 * q)
        idx = jnp.where(q < 2, view1, 6 + q + 2 * p)
        return cen[idx, 128 * h : 128 * h + 128]

    lax.fori_loop(0, 4, norm, 0)
    chain(3)
    lax.fori_loop(4, 8, norm, 0)

    fa = ab(2 * c + lax.div(z, 4))
    fk = kb(lax.rem(z, 4))
    pad = jnp.zeros((7, 256), F32)
    ra = jnp.concatenate([fin[fa, 1:2, :] * (2.0 * LAMBDA / BATCH), pad], 0)
    rk = jnp.concatenate([fin[fk, 1:2, :], pad], 0)
    rows_id = lax.broadcasted_iota(jnp.int32, (256, 256), 0)
    cols_id = lax.broadcasted_iota(jnp.int32, (256, 256), 1)
    off = rows_id + (c + z) * 256 != cols_id
    scl[...] = jnp.where(off, tn(ra, rk, HIGH), 0.0)
    mu_a = [(st2m[0, 8] if s == 0 else st2[s - 1, 8]) - fin[fa, 2:3, :] for s in range(8)]
    mu_k = [(st2m[0, 9] if s == 0 else st2[s - 1, 9]) - fin[fk, 2:3, :] for s in range(8)]
    fix[...] = scl[...] * tn(jnp.concatenate(mu_a, 0) * 256.0, jnp.concatenate(mu_k, 0), HIGH)
    chain(4)

    for n in range(4):
        acc1[n] = jnp.zeros((512, 256), F32)
        acc2[n] = jnp.zeros((512, 256), F32)
    rsq[...] = jnp.zeros_like(rsq)
    csq[...] = jnp.zeros_like(csq)

    c_recv(7)
    g_in = {}
    for u in range(2):
        rows = slice(128 * u, 128 * u + 128)
        v = cown[7, rows] + crecv[7, rows].astype(F32)
        for d in range(2):
            z_in[(d, 4, u)].wait_recv()
            v = v + zr[zslot(d, 4, u)].astype(F32)
        g[c, z, u] = (v * scl[rows] + fix[rows]).astype(BF16)
        for d in range(2):
            i = zslot(d, 1, u)
            send(M_ZG + i, g.at[c, z, u], g.at[c, z, u], zto[d])
        send(M_GD + 14 + u, g.at[c, z, u], g.at[c, z, u], core)

    def gather_step(t, last):
        for u in range(2):
            for d in range(2):
                if last and u != d:
                    continue
                i = d * 8 + (t - 1) * 2 + u
                source = lax.rem(z + (8 - t if d == 0 else t), 8)
                part = g.at[c, source, u]
                make(M_ZG + i, part, part, zto[d]).wait_recv()
                if not last:
                    onward = make(M_ZG + i + 2, part, part, zto[d])
                    if u == d:
                        onward.start()
                    else:
                        pl.when(t < 3)(onward.start)
                make(M_GD + (d * 7 + 6 if last else d * 7 + (t - 1) * 2 + u), part, part, core).start()

    def use(j, zs_):
        a = 2 * j + lax.div(zs_, 4)
        k = lax.rem(zs_, 4)
        ga = g[j, zs_].reshape(256, 256)
        acc1[a] += nt(nrm[kb(k)], ga)
        acc2[k] += nn(nrm[ab(a)], ga)
        v = ga.astype(F32)
        s = v * v
        rsq[a] += s[:, 0:128] + s[:, 128:256]
        csq[k] += jnp.sum(s.reshape(32, 8, 256), 0)

    def from_core(i):
        part = g.at[0, 0, 0]
        make(M_GD + i, part, part, core).wait_recv()

    use(c, z)
    from_core(14)
    from_core(15)
    use(1 - c, z)

    def step(t, carry):
        gather_step(t, False)

        def two(n, inner):
            use(c, lax.rem(z + (8 - t) + n * 2 * t, 8))
            return inner

        lax.fori_loop(0, 2, two, 0)

        def two_other(n, inner):
            for u in range(2):
                from_core(n * 7 + (t - 1) * 2 + u)
            use(1 - c, lax.rem(z + (8 - t) + n * 2 * t, 8))
            return inner

        lax.fori_loop(0, 2, two_other, 0)
        return carry

    lax.fori_loop(1, 4, step, 0)
    gather_step(4, True)

    def final_two(n, carry):
        use(lax.rem(c + n, 2), lax.rem(z + 4, 8))
        return carry

    from_core(6)
    from_core(13)
    lax.fori_loop(0, 2, final_two, 0)

    for a in range(4):
        rowsq[a] = nt(jnp.ones((8, 128), F32), rsq[a], HIGH) * (0.5 / LAMBDA)
        colsq[a] = jnp.sum(csq[a], 0, keepdims=True) * (0.5 / LAMBDA)

    def partial1(a, o):
        b = AB[a]
        rows = slice(o * 256, o * 256 + 256)
        f = nrm[b, rows].astype(F32)
        v = acc1[a, rows] - f * rowsq[a, 0:1, :]
        if a == 0:
            v = v + (nrm[2, rows].astype(F32) - f * fin[8, 0:1, :]) * fin[8, 1:2, :]
        return v * fin[b, 1:2, :]

    def partial2(k, o):
        b = KB[k]
        rows = slice(o * 256, o * 256 + 256)
        s = nrm[b, rows].astype(F32)
        v = acc2[k, rows] - s * colsq[k]
        if k == 0:
            v = v + (nrm[0, rows].astype(F32) - s * fin[8, 0:1, :]) * fin[8, 1:2, :]
        return v * fin[b, 1:2, :]

    p2[2, 0] = partial2(2, 0).astype(BF16)
    relay2 = [send(M_P2O + 0, p2.at[2, 0], p2relay.at[0], right)]
    p2[2, 1] = partial2(2, 1).astype(BF16)
    relay2.append(send(M_P2O + 1, p2.at[2, 1], p2relay.at[1], left))
    p1[0, 2] = partial1(2, 0).astype(BF16)
    relay1 = [send(M_P1O + 0, p1.at[0, 2], p1relay.at[0], sib)]
    p1[0, 3] = partial1(3, 0).astype(BF16)
    relay1.append(send(M_P1O + 1, p1.at[0, 3], p1relay.at[1], non))
    p2[1, 1] = partial2(1, 1).astype(BF16)
    in2 = [send(M_P2R + 1, p2.at[1, 1], p2in.at[0, 1], right)]
    p2[3, 0] = partial2(3, 0).astype(BF16)
    in2.append(send(M_P2L + 0, p2.at[3, 0], p2in.at[1, 0], left))
    p1[1, 2] = partial1(2, 1).astype(BF16)
    in1 = [send(M_P1N + 1, p1.at[1, 2], p1in.at[1, 1], non)]
    p1[1, 1] = partial1(1, 1).astype(BF16)
    in1.append(send(M_P1S + 0, p1.at[1, 1], p1in.at[0, 0], sib))
    v1 = partial2(1, 0)
    relay2[0].wait_recv()
    p2[1, 0] = (v1 + p2relay[0].astype(F32)).astype(BF16)
    in2.append(send(M_P2R + 0, p2.at[1, 0], p2in.at[0, 0], right))
    v3 = partial2(3, 1)
    relay2[1].wait_recv()
    p2[3, 1] = (v3 + p2relay[1].astype(F32)).astype(BF16)
    in2.append(send(M_P2L + 1, p2.at[3, 1], p2in.at[1, 1], left))
    v = partial1(3, 1)
    relay1[0].wait_recv()
    p1[1, 3] = (v + p1relay[0].astype(F32)).astype(BF16)
    in1.append(send(M_P1N + 0, p1.at[1, 3], p1in.at[1, 0], non))
    v = partial1(0, 1)
    relay1[1].wait_recv()
    p1[1, 0] = (v + p1relay[1].astype(F32)).astype(BF16)
    in1.append(send(M_P1S + 1, p1.at[1, 0], p1in.at[0, 1], sib))

    ob1[0] = partial1(0, 0)
    ob1[1] = partial1(1, 0)
    ob2[0] = partial2(0, 1)
    ob2[1] = partial2(0, 0)
    for cp in in2:
        cp.wait_recv()
    xs[...] = (ob2[0] + p2in[0, 1].astype(F32) + p2in[1, 1].astype(F32)).astype(BF16)
    x_in = send(M_X, xs, xr, sib)
    outs = []

    def put(src, ref, col, i):
        cp = pltpu.make_async_copy(src, ref.at[:, pl.ds(pl.multiple_of(col, 256), 256)], os_.at[i])
        cp.start()
        outs.append(cp)

    ob2[1] = ob2[1] + p2in[0, 0].astype(F32) + p2in[1, 0].astype(F32)
    put(ob2.at[1], out2, lo, 0)
    for cp in in1:
        cp.wait_recv()
    for e in range(2):
        ob1[e] = ob1[e] + p1in[0, e].astype(F32) + p1in[1, e].astype(F32)
        put(ob1.at[e], out1, lo if e == 0 else hi, 1 + e)
    x_in.wait_recv()
    ob2[0] = xr[...].astype(F32)
    put(ob2.at[0], out2, hi, 3)
    for cp in outs:
        cp.wait()
    for cp in sends:
        cp.wait_send()

    def sent(i, part):
        make(i, part, part, core).wait_send()

    for s in range(8):
        sent(M_C + s, csend.at[s])
    for d in range(2):
        for t in range(2, 5):
            for u in range(2):
                if t < 4 or u == d:
                    sent(M_ZG + zslot(d, t, u), g.at[0, 0, 0])
    for i in range(14):
        sent(M_GD + i, g.at[0, 0, 0])


def body(first, second):
    v = pltpu.VMEM
    out = jax.ShapeDtypeStruct((256, 512), F32)
    anywhere = pl.BlockSpec(memory_space=pl.ANY)
    return pl.pallas_call(
        kernel,
        out_shape=(out, out),
        in_specs=[anywhere, anywhere],
        out_specs=(anywhere, anywhere),
        scratch_shapes=[
            v((12, 256, 256), F32),
            v((12, 256, 256), BF16),
            v((8, 256, 256), BF16),
            v((2, 4, 256, 256), BF16),
            v((12, 4, 256), F32),
            v((2, 4, 4, 256), F32),
            v((4, 8, 4, 256), F32),
            v((8, 10, 4, 256), F32),
            v((7, 10, 4, 256), F32),
            v((9, 4, 256), F32),
            v((256, 256), F32),
            v((256, 256), F32),
            v((8, 512, 256), BF16),
            v((8, 256, 256), F32),
            v((8, 256, 256), BF16),
            v((8, 256, 256), BF16),
            v((16, 128, 256), BF16),
            v((16, 128, 256), BF16),
            v((2, 8, 2, 128, 256), BF16),
            v((4, 512, 256), F32),
            v((4, 512, 256), F32),
            v((4, 256, 128), F32),
            v((4, 8, 256), F32),
            v((4, 8, 256), F32),
            v((4, 1, 256), F32),
            v((2, 4, 256, 256), BF16),
            v((2, 2, 256, 256), BF16),
            v((2, 256, 256), BF16),
            v((4, 2, 256, 256), BF16),
            v((2, 2, 256, 256), BF16),
            v((2, 256, 256), BF16),
            v((256, 256), BF16),
            v((256, 256), BF16),
            v((2, 256, 256), F32),
            v((2, 256, 256), F32),
            pltpu.SemaphoreType.DMA((M_ALL,)),
            pltpu.SemaphoreType.DMA((M_ALL,)),
            pltpu.SemaphoreType.DMA((12,)),
            pltpu.SemaphoreType.DMA((4,)),
        ],
        compiler_params=pltpu.CompilerParams(
            collective_id=0, has_side_effects=True, vmem_limit_bytes=56 * 1024 * 1024
        ),
    )(first, second)


def solution(mesh):
    return jax.shard_map(
        body,
        mesh=mesh,
        in_specs=(P("dp", None), P("dp", None)),
        out_specs=(P("dp", "replica"), P("dp", "replica")),
        check_vma=False,
    )
```

time: 599 us -> 82.5 us (0.14)
  blocking collectives: 341 us -> 0 us
  waiting for transfers between devices: 180 us -> 0 us
  Pallas kernels: 0 us -> 78 us
  other arithmetic: 23.2 us -> 0 us
  matrix products: 15.3 us -> 0 us
  between operations: 13.9 us -> 0.64 us
  local copies, waits for them, and re-layouts: 16.7 us -> 3.74 us
  starting transfers between devices: 8.22 us -> 0 us
    psum x3 -> x0, blocking collectives: 268 us -> none  [the longest x1 108 us: body(): totals = lax.psum((jnp.sum(first_view, 0), jnp.sum(second_view, 0)), 'dp')]
    reduce_scatter x1 -> x0, waiting for transfers between devices: 78.4 us -> none  [body(): lax.psum_scatter(first_rows.astype(jnp.bfloat16), 'replica', scatter_dime...]
    pallas_call x0 -> x1, Pallas kernels: none -> 78 us  [body(): pl.pallas_call(kernel, out_shape=(out, out), in_specs=[anywhere, anywhere...]
    all_to_all x1 -> x0, blocking collectives: 72.9 us -> none  [body(): lax.all_to_all(first_full.astype(jnp.bfloat16), 'dp', split_axis=0, conca...]
    all_to_all x1 -> x0, waiting for transfers between devices: 72.7 us -> none  [body(): lax.all_to_all(sent_first, 'dp', split_axis=1, concat_axis=0, tiled=True)]
    all_gather x2 -> x0, waiting for transfers between devices: 28.7 us -> none  [the longest x1 21.8 us: body(): gathered = lax.all_gather(own_second, 'dp', axis=0, tiled=True)]
    dot_general x3 -> x0, matrix products: 15.3 us -> none  [the longest x1 5.81 us: body(): lax.dot_general(gathered, grad_block, (((1,), (1,)), ((), ())), preferred...]
    reduce_sum x5 -> x0, other arithmetic: 10.2 us -> none  [the longest x2 4.79 us: body(): totals = lax.psum((jnp.sum(first_view, 0), jnp.sum(second_view, 0)), 'dp')]
  transfers between devices with their start and end apart: 4 -> 0, of which waited for: 4 -> 0; matrix products, arithmetic and copies ran while one was open for 4% -> 0% of each run, Pallas kernels for 0% -> 0%
where the time goes in v1:
time: 82.5 us; the launch traced here: 82.4 us
  Pallas kernels  78 us (95%)
  local copies, waits for them, and re-layouts  3.74 us (5%)
    pallas_call x1, Pallas kernels, body(): pl.pallas_call(kernel, out_shape=(out, out), in_specs=[anywhere, anywhere...  78 us
    unnamed x2, local copies, waits for them, and re-layouts  3.74 us

profile of v1, /device:TPU:1, one launch (start us, length us, event | category | flops | bytes accessed | tf_op | source)
XLA Modules:
  0.0 82.4 jit_solution(5650400887381488465)
XLA Ops:
  0.6 78.0 %shard_map.41 = (f32[256,512]{1,0:T(8,128)}, f32[256,512]{1,0:T(8,128)}) custom-call(f32[256,4096]{1,0:T(8,128)} %first.1, f32[256,4096]{1,0:T(8,128)} %second.1), custom_call_target="tpu_custom_call" | custom-call | tf_op jit(solution)/shard_map/pallas_call | solution.py:515
  78.6 1.9 %copy.6 = f32[256,512]{1,0:T(8,128)} copy(f32[256,512]{1,0:T(8,128)} %get-tuple-element.4) | data formatting | bytes 1048576
  80.5 1.9 %copy.7 = f32[256,512]{1,0:T(8,128)} copy(f32[256,512]{1,0:T(8,128)} %get-tuple-element.5) | data formatting | bytes 1048576

commit v2 on v1

--- a/solution.py
+++ b/solution.py
@@ -12,27 +12,27 @@
 BF16 = jnp.bfloat16
 BATCH = 8192
 
-OWN = (2, 1, 8, 9, 3, 7, 10, 11)
-STAT_SIB = (1, 2, 0, 4)
-STAT_NON = (1, 2, 5, 6)
+OWN = (3, 2, 9, 10, 7, 8, 11, 12)
+STAT_SIB = (2, 3, 0, 4)
+STAT_NON = (2, 3, 5, 6)
 KB = (2, 3, 6, 7)
 AB = (0, 1, 4, 5)
 
 M_Y = 0
-M_ST1 = 11
-M_ST2 = 16
-M_C = 23
-M_ZR = 31
-M_ZG = 47
-M_GD = 63
-M_P1O = 79
-M_P1S = 81
-M_P1N = 83
-M_P2O = 85
-M_P2R = 87
-M_P2L = 89
-M_X = 91
-M_ALL = 92
+M_ST1 = 12
+M_ST2 = 17
+M_C = 24
+M_ZR = 32
+M_ZG = 48
+M_GD = 64
+M_P1O = 84
+M_P1S = 86
+M_P1N = 88
+M_P2O = 90
+M_P2R = 94
+M_P2L = 98
+M_X = 102
+M_ALL = 103
 
 HIGH = lax.Precision.HIGHEST
 
@@ -100,14 +100,15 @@
     hi = 256 - lo
     loads = [
         load(0, second, base + pieces[0] + hi),
-        load(1, first, base + mine + hi),
-        load(2, first, base + mine + lo),
-        load(3, first, 2048 - base + mine + lo),
+        load(1, second, 2048 - base + pieces[0] + hi),
+        load(2, first, base + mine + hi),
+        load(3, first, base + mine + lo),
         load(4, second, base + pieces[1] + hi),
         load(5, second, 2048 - base + pieces[2] + hi),
         load(6, second, 2048 - base + pieces[3] + hi),
-        load(7, first, 2048 - base + mine + hi),
-    ] + [load(8 + k, second, base + pieces[k] + lo) for k in range(4)]
+        load(7, first, 2048 - base + mine + lo),
+        load(8, first, 2048 - base + mine + hi),
+    ] + [load(9 + k, second, base + pieces[k] + lo) for k in range(4)]
     for cp in loads:
         cp.start()
 
@@ -143,20 +144,18 @@
         return carry
 
     top, low = pl.ds(0, 128), pl.ds(128, 128)
-    lax.fori_loop(0, 1, local_stats, 0)
+    lax.fori_loop(0, 2, local_stats, 0)
     pl.semaphore_wait(barrier, len(partners))
-    yk0 = send(M_Y + 0, cen.at[0], oth.at[2], sib)
-    lax.fori_loop(1, 4, local_stats, 0)
-    xin0 = [
-        send(M_Y + 1, cen.at[1], oth.at[0], sib),
-        send(M_Y + 2, cen.at[1], oth.at[4], non),
+    y_top = send(M_Y + 0, cen.at[0, top], oth.at[2, top], sib)
+    y_low = send(M_Y + 1, cen.at[1, low], oth.at[2, low], non)
+    lax.fori_loop(2, 4, local_stats, 0)
+    x_in = [
+        send(M_Y + 2, cen.at[2], oth.at[0], sib),
+        send(M_Y + 3, cen.at[2], oth.at[4], non),
+        send(M_Y + 4, cen.at[3], oth.at[1], sib),
+        send(M_Y + 5, cen.at[3], oth.at[5], non),
     ]
-    xin1 = [
-        send(M_Y + 3, cen.at[2, top], oth.at[1, top], sib),
-        send(M_Y + 4, cen.at[3, low], oth.at[1, low], non),
-    ]
-    xin2 = [send(M_Y + 5, cen.at[2], oth.at[5], non)]
-    lax.fori_loop(4, 12, local_stats, 0)
+    lax.fori_loop(4, 13, local_stats, 0)
 
     def comoment(i, j):
         return jnp.sum((raw[i] - stat[i, 0:1, :]) * (raw[j] - stat[j, 0:1, :]), 0, keepdims=True)
@@ -166,8 +165,8 @@
         smsg[1, n] = stat[STAT_NON[n]]
     for b in range(8):
         st1[0, b] = stat[OWN[b]]
-    smsg[0, 0, 3:4, :] = comoment(1, 0)
-    st1[0, 0, 3:4, :] = comoment(2, 8)
+    smsg[0, 0, 3:4, :] = comoment(2, 0)
+    st1[0, 0, 3:4, :] = comoment(3, 9)
     st_in = [
         send(M_ST1 + 0, smsg.at[0], st1.at[2, pl.ds(0, 4)], sib),
         send(M_ST1 + 1, smsg.at[1], st1.at[2, pl.ds(4, 4)], non),
@@ -175,17 +174,21 @@
         send(M_ST1 + 3, smsg.at[1], st1.at[3, pl.ds(4, 4)], nonc),
         send(M_ST1 + 4, st1.at[0], st1.at[1], core),
     ]
-    yk0.wait_recv()
-    yk1 = send(M_Y + 6, oth.at[2], oth.at[3], left)
-    yk3 = send(M_Y + 7, oth.at[2], oth.at[7], right)
+    y_top.wait_recv()
+    t1 = send(M_Y + 6, oth.at[2, top], oth.at[3, top], left)
+    t3 = send(M_Y + 7, oth.at[2, top], oth.at[7, top], right)
+    y_low.wait_recv()
+    l1 = send(M_Y + 8, oth.at[2, low], oth.at[3, low], left)
+    l3 = send(M_Y + 9, oth.at[2, low], oth.at[7, low], right)
     for a in range(4):
         xt[0, a] = cen[OWN[AB[a]]].T
+    t1.wait_recv()
+    yk2 = [send(M_Y + 10, oth.at[3, top], oth.at[6, top], left)]
+    t3.wait_recv()
+    l3.wait_recv()
+    yk2.append(send(M_Y + 11, oth.at[7, low], oth.at[6, low], right))
     for cp in st_in:
         cp.wait_recv()
-    yk1.wait_recv()
-    yk2 = [send(M_Y + 8, oth.at[3, top], oth.at[6, top], left)]
-    yk3.wait_recv()
-    yk2.append(send(M_Y + 9, oth.at[7, low], oth.at[6, low], right))
 
     def merge(rows_of, slots, count):
         devs = []
@@ -217,11 +220,15 @@
             st2m[q, 9, s : s + 1, :] = st1[s, fk, 0:1, :]
     st2_in = [send(M_ST2 + q - 1, st2m.at[q], st2.at[q - 1], zdev[q]) for q in range(1, 8)]
 
-    for cps, a in ((xin0, (0, 2)), (xin1, (1,)), (xin2, (3,))):
-        for cp in cps:
-            cp.wait_recv()
-        for n in a:
-            xt[1, n] = oth[AB[n]].T
+    for n in range(4):
+        acc1[n] = jnp.zeros((512, 256), F32)
+        acc2[n] = jnp.zeros((512, 256), F32)
+    rsq[...] = jnp.zeros_like(rsq)
+    csq[...] = jnp.zeros_like(csq)
+    for cp, n in zip(x_in, (0, 2, 1, 3)):
+        cp.wait_recv()
+        xt[1, n] = oth[AB[n]].T
+    l1.wait_recv()
     for cp in yk2:
         cp.wait_recv()
 
@@ -230,7 +237,7 @@
         d = lax.rem(z + r, 8)
         i = lax.div(d, 4)
         k = lax.rem(d, 4)
-        y0 = cen[8 + k]
+        y0 = cen[9 + k]
         y1 = oth[kb(k)]
         a = 2 * (1 - c) + i
         csend[s] = (nn(xt[0, a], y0) + nn(xt[1, a], y1)).astype(BF16)
@@ -247,29 +254,32 @@
 
     z_in = {}
 
-    def chain(t):
+    def chain(t, far):
         dist = 5 - t
-        slot = (8 - 2 * dist - 1, 8 - 2 * dist) if dist < 4 else (0, 0)
+        slot = (7 - 2 * dist, 8 - 2 * dist) if dist < 4 else (0, 0)
+        if (t, far) in ((1, True), (2, False), (3, False), (4, False)):
+            c_recv(slot[0])
+            if t > 1:
+                c_recv(slot[1])
         for d in range(2):
-            if t > 1 or d == 0:
-                c_recv(slot[d])
-        for u in range(2):
-            for d in range(2):
-                if t == 1 and u != d:
-                    continue
-                n = slot[d]
-                v = cown[n, 128 * u : 128 * u + 128] + crecv[n, 128 * u : 128 * u + 128].astype(F32)
-                if (d, t - 1, u) in z_in:
-                    z_in[(d, t - 1, u)].wait_recv()
-                    v = v + zr[zslot(d, t - 1, u)].astype(F32)
-                i = zslot(d, t, u)
-                zs[i] = v.astype(BF16)
-                z_in[(d, t, u)] = send(M_ZR + i, zs.at[i], zr.at[i], zto[d])
+            u = d if far else 1 - d
+            n = slot[d]
+            rows = slice(128 * u, 128 * u + 128)
+            v = cown[n, rows] + crecv[n, rows].astype(F32)
+            if (d, t - 1, u) in z_in:
+                z_in[(d, t - 1, u)].wait_recv()
+                v = v + zr[zslot(d, t - 1, u)].astype(F32)
+            i = zslot(d, t, u)
+            zs[i] = v.astype(BF16)
+            z_in[(d, t, u)] = send(M_ZR + i, zs.at[i], zr.at[i], zto[d])
 
     lax.fori_loop(0, 3, corr, 0)
-    chain(1)
-    lax.fori_loop(3, 8, corr, 0)
-    chain(2)
+    chain(1, True)
+    chain(2, False)
+    lax.fori_loop(3, 5, corr, 0)
+    chain(2, True)
+    lax.fori_loop(5, 8, corr, 0)
+    chain(3, False)
 
     for cp in st2_in:
         cp.wait_recv()
@@ -301,12 +311,12 @@
     def own_block(b, h):
         p = lax.div(b, 4)
         q = lax.rem(b, 4)
-        view1 = jnp.where(p == 0, 2 - q, 3 + 4 * q)
-        idx = jnp.where(q < 2, view1, 6 + q + 2 * p)
+        idx = jnp.where(q < 2, jnp.where(p == 0, 3 - q, 7 + q), 7 + q + 2 * p)
         return cen[idx, 128 * h : 128 * h + 128]
 
+    chain(3, True)
     lax.fori_loop(0, 4, norm, 0)
-    chain(3)
+    chain(4, False)
     lax.fori_loop(4, 8, norm, 0)
 
     fa = ab(2 * c + lax.div(z, 4))
@@ -321,44 +331,35 @@
     mu_a = [(st2m[0, 8] if s == 0 else st2[s - 1, 8]) - fin[fa, 2:3, :] for s in range(8)]
     mu_k = [(st2m[0, 9] if s == 0 else st2[s - 1, 9]) - fin[fk, 2:3, :] for s in range(8)]
     fix[...] = scl[...] * tn(jnp.concatenate(mu_a, 0) * 256.0, jnp.concatenate(mu_k, 0), HIGH)
-    chain(4)
-
-    for n in range(4):
-        acc1[n] = jnp.zeros((512, 256), F32)
-        acc2[n] = jnp.zeros((512, 256), F32)
-    rsq[...] = jnp.zeros_like(rsq)
-    csq[...] = jnp.zeros_like(csq)
+    chain(4, True)
 
     c_recv(7)
-    g_in = {}
     for u in range(2):
         rows = slice(128 * u, 128 * u + 128)
         v = cown[7, rows] + crecv[7, rows].astype(F32)
-        for d in range(2):
+        for d in (1 - u, u):
             z_in[(d, 4, u)].wait_recv()
             v = v + zr[zslot(d, 4, u)].astype(F32)
         g[c, z, u] = (v * scl[rows] + fix[rows]).astype(BF16)
-        for d in range(2):
+        for d in (u, 1 - u):
             i = zslot(d, 1, u)
             send(M_ZG + i, g.at[c, z, u], g.at[c, z, u], zto[d])
-        send(M_GD + 14 + u, g.at[c, z, u], g.at[c, z, u], core)
-
-    def gather_step(t, last):
-        for u in range(2):
-            for d in range(2):
-                if last and u != d:
-                    continue
-                i = d * 8 + (t - 1) * 2 + u
-                source = lax.rem(z + (8 - t if d == 0 else t), 8)
-                part = g.at[c, source, u]
-                make(M_ZG + i, part, part, zto[d]).wait_recv()
-                if not last:
-                    onward = make(M_ZG + i + 2, part, part, zto[d])
-                    if u == d:
-                        onward.start()
-                    else:
-                        pl.when(t < 3)(onward.start)
-                make(M_GD + (d * 7 + 6 if last else d * 7 + (t - 1) * 2 + u), part, part, core).start()
+        send(M_GD + u, g.at[c, z, u], g.at[c, z, u], core)
+
+    def arrive(t, far, onward):
+        for d in range(2):
+            u = d if far else 1 - d
+            i = d * 8 + (t - 1) * 2 + u
+            source = lax.rem(z + (8 - t if d == 0 else t), 8)
+            part = g.at[c, source, u]
+            make(M_ZG + i, part, part, zto[d]).wait_recv()
+            if onward is not None:
+                start = make(M_ZG + i + 2, part, part, zto[d]).start
+                if onward is True:
+                    start()
+                else:
+                    pl.when(onward)(start)
+            make(M_GD + 4 * t + 2 * d + u, part, part, core).start()
 
     def use(j, zs_):
         a = 2 * j + lax.div(zs_, 4)
@@ -371,43 +372,41 @@
         rsq[a] += s[:, 0:128] + s[:, 128:256]
         csq[k] += jnp.sum(s.reshape(32, 8, 256), 0)
 
-    def from_core(i):
+    def from_core(t, d, u):
         part = g.at[0, 0, 0]
-        make(M_GD + i, part, part, core).wait_recv()
-
-    use(c, z)
-    from_core(14)
-    from_core(15)
-    use(1 - c, z)
+        make(M_GD + 4 * t + 2 * d + u, part, part, core).wait_recv()
+
+    def uses(t, mine_too):
+        def one(n, inner):
+            if not mine_too:
+                for u in range(2):
+                    from_core(t, n, u)
+            use(c if mine_too else 1 - c, lax.rem(z + (8 - t) + n * 2 * t, 8))
+            return inner
+
+        lax.fori_loop(0, jnp.where(t == 0, 1, 2), one, 0)
+
+    uses(0, True)
 
     def step(t, carry):
-        gather_step(t, False)
-
-        def two(n, inner):
-            use(c, lax.rem(z + (8 - t) + n * 2 * t, 8))
-            return inner
-
-        lax.fori_loop(0, 2, two, 0)
-
-        def two_other(n, inner):
-            for u in range(2):
-                from_core(n * 7 + (t - 1) * 2 + u)
-            use(1 - c, lax.rem(z + (8 - t) + n * 2 * t, 8))
-            return inner
-
-        lax.fori_loop(0, 2, two_other, 0)
+        arrive(t, True, True)
+        uses(t - 1, False)
+        arrive(t, False, t < 3)
+        uses(t, True)
         return carry
 
     lax.fori_loop(1, 4, step, 0)
-    gather_step(4, True)
+    uses(3, False)
+    arrive(4, True, None)
 
     def final_two(n, carry):
         use(lax.rem(c + n, 2), lax.rem(z + 4, 8))
         return carry
 
-    from_core(6)
-    from_core(13)
-    lax.fori_loop(0, 2, final_two, 0)
+    lax.fori_loop(0, 1, final_two, 0)
+    from_core(4, 0, 0)
+    from_core(4, 1, 1)
+    lax.fori_loop(1, 2, final_two, 0)
 
     for a in range(4):
         rowsq[a] = nt(jnp.ones((8, 128), F32), rsq[a], HIGH) * (0.5 / LAMBDA)
@@ -431,47 +430,57 @@
             v = v + (nrm[0, rows].astype(F32) - s * fin[8, 0:1, :]) * fin[8, 1:2, :]
         return v * fin[b, 1:2, :]
 
-    p2[2, 0] = partial2(2, 0).astype(BF16)
-    relay2 = [send(M_P2O + 0, p2.at[2, 0], p2relay.at[0], right)]
-    p2[2, 1] = partial2(2, 1).astype(BF16)
-    relay2.append(send(M_P2O + 1, p2.at[2, 1], p2relay.at[1], left))
+    def p2_relay(o):
+        p2[2, o] = partial2(2, o).astype(BF16)
+        return [
+            send(M_P2O + 2 * o, p2.at[2, o, top], p2relay.at[o, top], right),
+            send(M_P2O + 2 * o + 1, p2.at[2, o, low], p2relay.at[o, low], left),
+        ]
+
+    def p2_send(o):
+        p2[1, o] = partial2(1, o).astype(BF16)
+        a = send(M_P2R + 2 * o, p2.at[1, o, low], p2in.at[0, o, low], right)
+        p2[3, o] = partial2(3, o).astype(BF16)
+        return [a, send(M_P2L + 2 * o, p2.at[3, o, top], p2in.at[1, o, top], left)]
+
+    def p2_add(o, relay):
+        relay[0].wait_recv()
+        p2[1, o, top] = (p2[1, o, top].astype(F32) + p2relay[o, top].astype(F32)).astype(BF16)
+        a = send(M_P2R + 2 * o + 1, p2.at[1, o, top], p2in.at[0, o, top], right)
+        relay[1].wait_recv()
+        p2[3, o, low] = (p2[3, o, low].astype(F32) + p2relay[o, low].astype(F32)).astype(BF16)
+        return [a, send(M_P2L + 2 * o + 1, p2.at[3, o, low], p2in.at[1, o, low], left)]
+
+    relay2 = p2_relay(1)
     p1[0, 2] = partial1(2, 0).astype(BF16)
     relay1 = [send(M_P1O + 0, p1.at[0, 2], p1relay.at[0], sib)]
     p1[0, 3] = partial1(3, 0).astype(BF16)
     relay1.append(send(M_P1O + 1, p1.at[0, 3], p1relay.at[1], non))
-    p2[1, 1] = partial2(1, 1).astype(BF16)
-    in2 = [send(M_P2R + 1, p2.at[1, 1], p2in.at[0, 1], right)]
-    p2[3, 0] = partial2(3, 0).astype(BF16)
-    in2.append(send(M_P2L + 0, p2.at[3, 0], p2in.at[1, 0], left))
+    in2 = p2_send(1)
+    relay20 = p2_relay(0)
     p1[1, 2] = partial1(2, 1).astype(BF16)
     in1 = [send(M_P1N + 1, p1.at[1, 2], p1in.at[1, 1], non)]
     p1[1, 1] = partial1(1, 1).astype(BF16)
     in1.append(send(M_P1S + 0, p1.at[1, 1], p1in.at[0, 0], sib))
-    v1 = partial2(1, 0)
-    relay2[0].wait_recv()
-    p2[1, 0] = (v1 + p2relay[0].astype(F32)).astype(BF16)
-    in2.append(send(M_P2R + 0, p2.at[1, 0], p2in.at[0, 0], right))
-    v3 = partial2(3, 1)
-    relay2[1].wait_recv()
-    p2[3, 1] = (v3 + p2relay[1].astype(F32)).astype(BF16)
-    in2.append(send(M_P2L + 1, p2.at[3, 1], p2in.at[1, 1], left))
-    v = partial1(3, 1)
-    relay1[0].wait_recv()
-    p1[1, 3] = (v + p1relay[0].astype(F32)).astype(BF16)
-    in1.append(send(M_P1N + 0, p1.at[1, 3], p1in.at[1, 0], non))
-    v = partial1(0, 1)
-    relay1[1].wait_recv()
-    p1[1, 0] = (v + p1relay[1].astype(F32)).astype(BF16)
-    in1.append(send(M_P1S + 1, p1.at[1, 0], p1in.at[0, 1], sib))
-
-    ob1[0] = partial1(0, 0)
-    ob1[1] = partial1(1, 0)
+    in2 += p2_add(1, relay2)
+    in20 = p2_send(0)
+    ob1[0] = partial1(3, 1)
+    ob1[1] = partial1(0, 1)
     ob2[0] = partial2(0, 1)
     ob2[1] = partial2(0, 0)
+    relay1[0].wait_recv()
+    p1[1, 3] = (ob1[0] + p1relay[0].astype(F32)).astype(BF16)
+    in1.append(send(M_P1N + 0, p1.at[1, 3], p1in.at[1, 0], non))
+    relay1[1].wait_recv()
+    p1[1, 0] = (ob1[1] + p1relay[1].astype(F32)).astype(BF16)
+    in20 += p2_add(0, relay20)
     for cp in in2:
         cp.wait_recv()
     xs[...] = (ob2[0] + p2in[0, 1].astype(F32) + p2in[1, 1].astype(F32)).astype(BF16)
     x_in = send(M_X, xs, xr, sib)
+    in1.append(send(M_P1S + 1, p1.at[1, 0], p1in.at[0, 1], sib))
+    ob1[0] = partial1(0, 0)
+    ob1[1] = partial1(1, 0)
     outs = []
 
     def put(src, ref, col, i):
@@ -479,6 +488,8 @@
         cp.start()
         outs.append(cp)
 
+    for cp in in20:
+        cp.wait_recv()
     ob2[1] = ob2[1] + p2in[0, 0].astype(F32) + p2in[1, 0].astype(F32)
     put(ob2.at[1], out2, lo, 0)
     for cp in in1:
@@ -500,29 +511,41 @@
     for s in range(8):
         sent(M_C + s, csend.at[s])
     for d in range(2):
-        for t in range(2, 5):
+        for t in range(1, 5):
             for u in range(2):
+                if t > 1 and (t < 4 or u == d):
+                    sent(M_ZG + zslot(d, t, u), g.at[0, 0, 0])
                 if t < 4 or u == d:
-                    sent(M_ZG + zslot(d, t, u), g.at[0, 0, 0])
-    for i in range(14):
-        sent(M_GD + i, g.at[0, 0, 0])
+                    sent(M_GD + 4 * t + 2 * d + u, g.at[0, 0, 0])
+
+
+def write_kernel(a, b, out1, out2, sem):
+    cps = []
+    for n, (src, dst) in enumerate(((a, out1), (b, out2))):
+        for q in range(4):
+            rows = pl.ds(64 * q, 64)
+            cps.append(pltpu.make_async_copy(src.at[rows], dst.at[rows], sem.at[4 * n + q]))
+    for cp in cps:
+        cp.start()
+    for cp in cps:
+        cp.wait()
 
 
 def body(first, second):
     v = pltpu.VMEM
     out = jax.ShapeDtypeStruct((256, 512), F32)
     anywhere = pl.BlockSpec(memory_space=pl.ANY)
-    return pl.pallas_call(
+    parts = pl.pallas_call(
         kernel,
         out_shape=(out, out),
         in_specs=[anywhere, anywhere],
         out_specs=(anywhere, anywhere),
         scratch_shapes=[
-            v((12, 256, 256), F32),
-            v((12, 256, 256), BF16),
+            v((13, 256, 256), F32),
+            v((13, 256, 256), BF16),
             v((8, 256, 256), BF16),
             v((2, 4, 256, 256), BF16),
-            v((12, 4, 256), F32),
+            v((13, 4, 256), F32),
             v((2, 4, 4, 256), F32),
             v((4, 8, 4, 256), F32),
             v((8, 10, 4, 256), F32),
@@ -555,13 +578,21 @@
             v((2, 256, 256), F32),
             pltpu.SemaphoreType.DMA((M_ALL,)),
             pltpu.SemaphoreType.DMA((M_ALL,)),
-            pltpu.SemaphoreType.DMA((12,)),
+            pltpu.SemaphoreType.DMA((13,)),
             pltpu.SemaphoreType.DMA((4,)),
         ],
         compiler_params=pltpu.CompilerParams(
             collective_id=0, has_side_effects=True, vmem_limit_bytes=56 * 1024 * 1024
         ),
     )(first, second)
+    return pl.pallas_call(
+        write_kernel,
+        out_shape=(out, out),
+        in_specs=[anywhere, anywhere],
+        out_specs=(anywhere, anywhere),
+        scratch_shapes=[pltpu.SemaphoreType.DMA((8,))],
+        compiler_params=pltpu.CompilerParams(vmem_limit_bytes=56 * 1024 * 1024),
+    )(*parts)
 
 
 def solution(mesh):

time: 82.5 us -> 112 us (1.36)
  Pallas kernels: 78 us -> 112 us
  local copies, waits for them, and re-layouts: 3.74 us -> 0 us
    pallas_call x0 -> x1, Pallas kernels: none -> 32.9 us  [body(): pl.pallas_call(write_kernel, out_shape=(out, out), in_specs=[anywhere, an...]
    unnamed x2 -> x0, local copies, waits for them, and re-layouts: 3.74 us -> none
where the time goes in v2:
time: 112 us
  Pallas kernels  112 us (100%)
    pallas_call x1, Pallas kernels, body(): pl.pallas_call(kernel, out_shape=(out, out), in_specs=[anywhere, anywhere...  78.8 us
    pallas_call x1, Pallas kernels, body(): pl.pallas_call(write_kernel, out_shape=(out, out), in_specs=[anywhere, an...  32.9 us

profile of v2, /device:TPU:1, one launch (start us, length us, event | category | flops | bytes accessed | tf_op | source)
XLA Modules:
  0.0 112.3 jit_solution(12004692157192207671)
XLA Ops:
  0.6 78.8 %shard_map.41 = (f32[256,512]{1,0:T(8,128)}, f32[256,512]{1,0:T(8,128)}) custom-call(f32[256,4096]{1,0:T(8,128)} %first.1, f32[256,4096]{1,0:T(8,128)} %second.1), custom_call_target="tpu_custom_call" | custom-call | tf_op jit(solution)/shard_map/pallas_call | solution.py:538
  79.4 32.9 %shard_map.42 = (f32[256,512]{1,0:T(8,128)}, f32[256,512]{1,0:T(8,128)}) custom-call(f32[256,512]{1,0:T(8,128)} %get-tuple-element.4.a, f32[256,512]{1,0:T(8,128)} %get-tuple-element.5.b), custom_call_target="tpu_custom_call" | custom-call | tf_op jit(solution)/shard_map/pallas_call | solution.py:588

commit v3 on v2

--- a/solution.py
+++ b/solution.py
@@ -12,9 +12,9 @@
 BF16 = jnp.bfloat16
 BATCH = 8192
 
-OWN = (3, 2, 9, 10, 7, 8, 11, 12)
-STAT_SIB = (2, 3, 0, 4)
-STAT_NON = (2, 3, 5, 6)
+OWN = (2, 3, 10, 11, 8, 9, 12, 13)
+STAT_SIB = (2, 3, 4, 5)
+STAT_NON = (2, 3, 6, 7)
 KB = (2, 3, 6, 7)
 AB = (0, 1, 4, 5)
 
@@ -25,14 +25,12 @@
 M_ZR = 32
 M_ZG = 48
 M_GD = 64
-M_P1O = 84
-M_P1S = 86
-M_P1N = 88
-M_P2O = 90
-M_P2R = 94
-M_P2L = 98
-M_X = 102
-M_ALL = 103
+M_P1 = 84
+M_P2O = 96
+M_P2R = 100
+M_P2L = 104
+M_X = 108
+M_ALL = 109
 
 HIGH = lax.Precision.HIGHEST
 
@@ -94,21 +92,26 @@
         )
 
     pieces = [lax.rem(x + k, 4) * 512 for k in range(4)]
+    kz = lax.rem(z, 4)
+    iz = lax.div(z, 4)
+    seed = lax.rem(x + kz, 4) * 512
     base = yhi * 2048
+    other = 2048 - base
     mine = x * 512
     lo = ylo * 256
     hi = 256 - lo
     loads = [
-        load(0, second, base + pieces[0] + hi),
-        load(1, second, 2048 - base + pieces[0] + hi),
-        load(2, first, base + mine + hi),
-        load(3, first, base + mine + lo),
-        load(4, second, base + pieces[1] + hi),
-        load(5, second, 2048 - base + pieces[2] + hi),
-        load(6, second, 2048 - base + pieces[3] + hi),
-        load(7, first, 2048 - base + mine + lo),
-        load(8, first, 2048 - base + mine + hi),
-    ] + [load(9 + k, second, base + pieces[k] + lo) for k in range(4)]
+        load(0, second, base + seed + hi),
+        load(1, second, other + seed + hi),
+        load(2, first, base + mine),
+        load(3, first, base + mine + 256),
+        load(4, second, base + pieces[0] + hi),
+        load(5, second, base + pieces[1] + hi),
+        load(6, second, other + pieces[2] + hi),
+        load(7, second, other + pieces[3] + hi),
+        load(8, first, other + mine),
+        load(9, first, other + mine + 256),
+    ] + [load(10 + k, second, base + pieces[k] + lo) for k in range(4)]
     for cp in loads:
         cp.start()
 
@@ -144,18 +147,21 @@
         return carry
 
     top, low = pl.ds(0, 128), pl.ds(128, 128)
+    k0, k1, k2, k3 = [kb(lax.rem(kz + n, 4)) for n in range(4)]
     lax.fori_loop(0, 2, local_stats, 0)
     pl.semaphore_wait(barrier, len(partners))
-    y_top = send(M_Y + 0, cen.at[0, top], oth.at[2, top], sib)
-    y_low = send(M_Y + 1, cen.at[1, low], oth.at[2, low], non)
+    y_top = send(M_Y + 0, cen.at[0, top], oth.at[k0, top], sib)
+    y_low = send(M_Y + 1, cen.at[1, low], oth.at[k0, low], non)
     lax.fori_loop(2, 4, local_stats, 0)
-    x_in = [
-        send(M_Y + 2, cen.at[2], oth.at[0], sib),
-        send(M_Y + 3, cen.at[2], oth.at[4], non),
-        send(M_Y + 4, cen.at[3], oth.at[1], sib),
-        send(M_Y + 5, cen.at[3], oth.at[5], non),
-    ]
-    lax.fori_loop(4, 13, local_stats, 0)
+    x_in = []
+    for n, e in enumerate((1 - iz, iz)):
+        x_in.append(
+            [
+                send(M_Y + 2 + 2 * n, cen.at[2 + e], oth.at[e], sib),
+                send(M_Y + 3 + 2 * n, cen.at[2 + e], oth.at[4 + e], non),
+            ]
+        )
+    lax.fori_loop(4, 14, local_stats, 0)
 
     def comoment(i, j):
         return jnp.sum((raw[i] - stat[i, 0:1, :]) * (raw[j] - stat[j, 0:1, :]), 0, keepdims=True)
@@ -165,8 +171,8 @@
         smsg[1, n] = stat[STAT_NON[n]]
     for b in range(8):
         st1[0, b] = stat[OWN[b]]
-    smsg[0, 0, 3:4, :] = comoment(2, 0)
-    st1[0, 0, 3:4, :] = comoment(3, 9)
+    smsg[0, 1 - ylo, 3:4, :] = comoment(3 - ylo, 4)
+    st1[0, ylo, 3:4, :] = comoment(2 + ylo, 10)
     st_in = [
         send(M_ST1 + 0, smsg.at[0], st1.at[2, pl.ds(0, 4)], sib),
         send(M_ST1 + 1, smsg.at[1], st1.at[2, pl.ds(4, 4)], non),
@@ -175,18 +181,13 @@
         send(M_ST1 + 4, st1.at[0], st1.at[1], core),
     ]
     y_top.wait_recv()
-    t1 = send(M_Y + 6, oth.at[2, top], oth.at[3, top], left)
-    t3 = send(M_Y + 7, oth.at[2, top], oth.at[7, top], right)
+    t1 = send(M_Y + 6, oth.at[k0, top], oth.at[k1, top], left)
+    t3 = send(M_Y + 7, oth.at[k0, top], oth.at[k3, top], right)
     y_low.wait_recv()
-    l1 = send(M_Y + 8, oth.at[2, low], oth.at[3, low], left)
-    l3 = send(M_Y + 9, oth.at[2, low], oth.at[7, low], right)
+    l1 = send(M_Y + 8, oth.at[k0, low], oth.at[k1, low], left)
+    l3 = send(M_Y + 9, oth.at[k0, low], oth.at[k3, low], right)
     for a in range(4):
         xt[0, a] = cen[OWN[AB[a]]].T
-    t1.wait_recv()
-    yk2 = [send(M_Y + 10, oth.at[3, top], oth.at[6, top], left)]
-    t3.wait_recv()
-    l3.wait_recv()
-    yk2.append(send(M_Y + 11, oth.at[7, low], oth.at[6, low], right))
     for cp in st_in:
         cp.wait_recv()
 
@@ -201,8 +202,9 @@
             m2 = total[1:2] + count * sum([d * d for d in dv[1:]], dv[0] * dv[0])
             devs.append(dv)
             res.append([m, m2, total[2:3], total[3:4]])
-        cross = sum([p * q for p, q in zip(devs[0][1:], devs[2][1:])], devs[0][0] * devs[2][0])
-        res[0][3] = res[0][3] + count * cross
+        for b in range(2):
+            cross = sum([p * q for p, q in zip(devs[b][1:], devs[2][1:])], devs[b][0] * devs[2][0])
+            res[b][3] = res[b][3] + count * cross
         return res
 
     for b, r in enumerate(merge(lambda s, b: st1[s, b], 4, 256.0)):
@@ -225,19 +227,24 @@
         acc2[n] = jnp.zeros((512, 256), F32)
     rsq[...] = jnp.zeros_like(rsq)
     csq[...] = jnp.zeros_like(csq)
-    for cp, n in zip(x_in, (0, 2, 1, 3)):
-        cp.wait_recv()
-        xt[1, n] = oth[AB[n]].T
-    l1.wait_recv()
-    for cp in yk2:
-        cp.wait_recv()
+    t1.wait_recv()
+    yk2 = [send(M_Y + 10, oth.at[k1, top], oth.at[k2, top], left)]
+    t3.wait_recv()
+    l3.wait_recv()
+    yk2.append(send(M_Y + 11, oth.at[k3, low], oth.at[k2, low], right))
+
+    def x_ready(n):
+        e = (1 - iz, iz)[n]
+        for j in range(2):
+            x_in[n][j].wait_recv()
+            xt[1, 2 * j + e] = oth[4 * j + e].T
 
     def corr(s, carry):
         r = jnp.where(lax.rem(s, 2) == 1, 4 - lax.div(s + 1, 2), 4 + lax.div(s, 2))
         d = lax.rem(z + r, 8)
         i = lax.div(d, 4)
         k = lax.rem(d, 4)
-        y0 = cen[9 + k]
+        y0 = cen[10 + k]
         y1 = oth[kb(k)]
         a = 2 * (1 - c) + i
         csend[s] = (nn(xt[0, a], y0) + nn(xt[1, a], y1)).astype(BF16)
@@ -273,9 +280,15 @@
             zs[i] = v.astype(BF16)
             z_in[(d, t, u)] = send(M_ZR + i, zs.at[i], zr.at[i], zto[d])
 
-    lax.fori_loop(0, 3, corr, 0)
+    x_ready(0)
+    lax.fori_loop(0, 1, corr, 0)
+    x_ready(1)
+    l1.wait_recv()
+    lax.fori_loop(1, 3, corr, 0)
     chain(1, True)
     chain(2, False)
+    for cp in yk2:
+        cp.wait_recv()
     lax.fori_loop(3, 5, corr, 0)
     chain(2, True)
     lax.fori_loop(5, 8, corr, 0)
@@ -292,7 +305,8 @@
         fin[b, 2:3, :] = r[0]
         fin[b, 3:4, :] = jnp.zeros_like(rstd)
         rstds.append(rstd)
-    cii = whole[0][3] * rstds[0] * rstds[2] * (1.0 / BATCH)
+    low_half = ylo == 0
+    cii = jnp.where(low_half, whole[0][3] * rstds[0], whole[1][3] * rstds[1]) * rstds[2] * (1.0 / BATCH)
     fin[8, 0:1, :] = cii
     fin[8, 1:2, :] = (-2.0 * (1.0 - cii)).astype(BF16).astype(F32)
 
@@ -311,7 +325,7 @@
     def own_block(b, h):
         p = lax.div(b, 4)
         q = lax.rem(b, 4)
-        idx = jnp.where(q < 2, jnp.where(p == 0, 3 - q, 7 + q), 7 + q + 2 * p)
+        idx = jnp.where(q < 2, 2 + q + 6 * p, 8 + q + 2 * p)
         return cen[idx, 128 * h : 128 * h + 128]
 
     chain(3, True)
@@ -326,7 +340,7 @@
     rk = jnp.concatenate([fin[fk, 1:2, :], pad], 0)
     rows_id = lax.broadcasted_iota(jnp.int32, (256, 256), 0)
     cols_id = lax.broadcasted_iota(jnp.int32, (256, 256), 1)
-    off = rows_id + (c + z) * 256 != cols_id
+    off = rows_id + jnp.where((c == 0) & (z == 4 * ylo), 0, 512) != cols_id
     scl[...] = jnp.where(off, tn(ra, rk, HIGH), 0.0)
     mu_a = [(st2m[0, 8] if s == 0 else st2[s - 1, 8]) - fin[fa, 2:3, :] for s in range(8)]
     mu_k = [(st2m[0, 9] if s == 0 else st2[s - 1, 9]) - fin[fk, 2:3, :] for s in range(8)]
@@ -395,8 +409,42 @@
         uses(t, True)
         return carry
 
+    def partial1(a, o):
+        b = ab(a)
+        rows = slice(o * 256, o * 256 + 256)
+        f = nrm[b, rows].astype(F32)
+        v = acc1[a, rows] - f * rowsq[a, 0:1, :]
+        gd = jnp.where(a == ylo, fin[8, 1:2, :], 0.0)
+        v = v + (nrm[2, rows].astype(F32) - f * fin[8, 0:1, :]) * gd
+        return v * fin[b, 1:2, :]
+
+    def p1_start(ph, e):
+        for a in (e, 2 + e):
+            rowsq[a] = nt(jnp.ones((8, 128), F32), rsq[a], HIGH) * (0.5 / LAMBDA)
+        m = M_P1 + 6 * ph
+        p1[ph, 0] = partial1(2 + e, 0).astype(BF16)
+        relay = [
+            send(m, p1.at[ph, 0, top], p1relay.at[ph, top], sib),
+            send(m + 1, p1.at[ph, 0, low], p1relay.at[ph, low], non),
+        ]
+        p1[ph, 1] = partial1(2 + e, 1).astype(BF16)
+        a = send(m + 2, p1.at[ph, 1, low], p1in.at[ph, 1, low], non)
+        p1[ph, 2] = partial1(e, 1).astype(BF16)
+        b = send(m + 3, p1.at[ph, 2, top], p1in.at[ph, 0, top], sib)
+        return relay, [a, b]
+
+    def p1_add(ph, relay):
+        m = M_P1 + 6 * ph
+        relay[0].wait_recv()
+        p1[ph, 1, top] = (p1[ph, 1, top].astype(F32) + p1relay[ph, top].astype(F32)).astype(BF16)
+        a = send(m + 4, p1.at[ph, 1, top], p1in.at[ph, 1, top], non)
+        relay[1].wait_recv()
+        p1[ph, 2, low] = (p1[ph, 2, low].astype(F32) + p1relay[ph, low].astype(F32)).astype(BF16)
+        return [a, send(m + 5, p1.at[ph, 2, low], p1in.at[ph, 0, low], sib)]
+
     lax.fori_loop(1, 4, step, 0)
     uses(3, False)
+    relay1, in1 = p1_start(0, iz)
     arrive(4, True, None)
 
     def final_two(n, carry):
@@ -408,18 +456,8 @@
     from_core(4, 1, 1)
     lax.fori_loop(1, 2, final_two, 0)
 
-    for a in range(4):
-        rowsq[a] = nt(jnp.ones((8, 128), F32), rsq[a], HIGH) * (0.5 / LAMBDA)
-        colsq[a] = jnp.sum(csq[a], 0, keepdims=True) * (0.5 / LAMBDA)
-
-    def partial1(a, o):
-        b = AB[a]
-        rows = slice(o * 256, o * 256 + 256)
-        f = nrm[b, rows].astype(F32)
-        v = acc1[a, rows] - f * rowsq[a, 0:1, :]
-        if a == 0:
-            v = v + (nrm[2, rows].astype(F32) - f * fin[8, 0:1, :]) * fin[8, 1:2, :]
-        return v * fin[b, 1:2, :]
+    for k in range(4):
+        colsq[k] = jnp.sum(csq[k], 0, keepdims=True) * (0.5 / LAMBDA)
 
     def partial2(k, o):
         b = KB[k]
@@ -427,7 +465,7 @@
         s = nrm[b, rows].astype(F32)
         v = acc2[k, rows] - s * colsq[k]
         if k == 0:
-            v = v + (nrm[0, rows].astype(F32) - s * fin[8, 0:1, :]) * fin[8, 1:2, :]
+            v = v + (nrm[ylo, rows].astype(F32) - s * fin[8, 0:1, :]) * fin[8, 1:2, :]
         return v * fin[b, 1:2, :]
 
     def p2_relay(o):
@@ -452,35 +490,23 @@
         return [a, send(M_P2L + 2 * o + 1, p2.at[3, o, low], p2in.at[1, o, low], left)]
 
     relay2 = p2_relay(1)
-    p1[0, 2] = partial1(2, 0).astype(BF16)
-    relay1 = [send(M_P1O + 0, p1.at[0, 2], p1relay.at[0], sib)]
-    p1[0, 3] = partial1(3, 0).astype(BF16)
-    relay1.append(send(M_P1O + 1, p1.at[0, 3], p1relay.at[1], non))
+    in1 += p1_add(0, relay1)
     in2 = p2_send(1)
+    relay1, more = p1_start(1, 1 - iz)
+    in1 += more
     relay20 = p2_relay(0)
-    p1[1, 2] = partial1(2, 1).astype(BF16)
-    in1 = [send(M_P1N + 1, p1.at[1, 2], p1in.at[1, 1], non)]
-    p1[1, 1] = partial1(1, 1).astype(BF16)
-    in1.append(send(M_P1S + 0, p1.at[1, 1], p1in.at[0, 0], sib))
     in2 += p2_add(1, relay2)
     in20 = p2_send(0)
-    ob1[0] = partial1(3, 1)
-    ob1[1] = partial1(0, 1)
     ob2[0] = partial2(0, 1)
     ob2[1] = partial2(0, 0)
-    relay1[0].wait_recv()
-    p1[1, 3] = (ob1[0] + p1relay[0].astype(F32)).astype(BF16)
-    in1.append(send(M_P1N + 0, p1.at[1, 3], p1in.at[1, 0], non))
-    relay1[1].wait_recv()
-    p1[1, 0] = (ob1[1] + p1relay[1].astype(F32)).astype(BF16)
+    in1 += p1_add(1, relay1)
     in20 += p2_add(0, relay20)
     for cp in in2:
         cp.wait_recv()
     xs[...] = (ob2[0] + p2in[0, 1].astype(F32) + p2in[1, 1].astype(F32)).astype(BF16)
-    x_in = send(M_X, xs, xr, sib)
-    in1.append(send(M_P1S + 1, p1.at[1, 0], p1in.at[0, 1], sib))
-    ob1[0] = partial1(0, 0)
-    ob1[1] = partial1(1, 0)
+    x_last = send(M_X, xs, xr, sib)
+    ob1[0] = partial1(iz, 0)
+    ob1[1] = partial1(1 - iz, 0)
     outs = []
 
     def put(src, ref, col, i):
@@ -494,10 +520,10 @@
     put(ob2.at[1], out2, lo, 0)
     for cp in in1:
         cp.wait_recv()
-    for e in range(2):
-        ob1[e] = ob1[e] + p1in[0, e].astype(F32) + p1in[1, e].astype(F32)
-        put(ob1.at[e], out1, lo if e == 0 else hi, 1 + e)
-    x_in.wait_recv()
+    for ph, e in enumerate((iz, 1 - iz)):
+        ob1[ph] = ob1[ph] + p1in[ph, 0].astype(F32) + p1in[ph, 1].astype(F32)
+        put(ob1.at[ph], out1, e * 256, 1 + ph)
+    x_last.wait_recv()
     ob2[0] = xr[...].astype(F32)
     put(ob2.at[0], out2, hi, 3)
     for cp in outs:
@@ -519,16 +545,20 @@
                     sent(M_GD + 4 * t + 2 * d + u, g.at[0, 0, 0])
 
 
-def write_kernel(a, b, out1, out2, sem):
+def write_kernel(a, b, out1, out2, held, sem_in, sem_out):
     cps = []
     for n, (src, dst) in enumerate(((a, out1), (b, out2))):
-        for q in range(4):
-            rows = pl.ds(64 * q, 64)
-            cps.append(pltpu.make_async_copy(src.at[rows], dst.at[rows], sem.at[4 * n + q]))
-    for cp in cps:
-        cp.start()
-    for cp in cps:
-        cp.wait()
+        for q in range(2):
+            i = 2 * n + q
+            rows = pl.ds(128 * q, 128)
+            come = pltpu.make_async_copy(src.at[rows], held.at[i], sem_in.at[i])
+            come.start()
+            cps.append((come, pltpu.make_async_copy(held.at[i], dst.at[rows], sem_out.at[i])))
+    for come, go in cps:
+        come.wait()
+        go.start()
+    for come, go in cps:
+        go.wait()
 
 
 def body(first, second):
@@ -541,11 +571,11 @@
         in_specs=[anywhere, anywhere],
         out_specs=(anywhere, anywhere),
         scratch_shapes=[
-            v((13, 256, 256), F32),
-            v((13, 256, 256), BF16),
+            v((14, 256, 256), F32),
+            v((14, 256, 256), BF16),
             v((8, 256, 256), BF16),
             v((2, 4, 256, 256), BF16),
-            v((13, 4, 256), F32),
+            v((14, 4, 256), F32),
             v((2, 4, 4, 256), F32),
             v((4, 8, 4, 256), F32),
             v((8, 10, 4, 256), F32),
@@ -566,7 +596,7 @@
             v((4, 8, 256), F32),
             v((4, 8, 256), F32),
             v((4, 1, 256), F32),
-            v((2, 4, 256, 256), BF16),
+            v((2, 3, 256, 256), BF16),
             v((2, 2, 256, 256), BF16),
             v((2, 256, 256), BF16),
             v((4, 2, 256, 256), BF16),
@@ -578,7 +608,7 @@
             v((2, 256, 256), F32),
             pltpu.SemaphoreType.DMA((M_ALL,)),
             pltpu.SemaphoreType.DMA((M_ALL,)),
-            pltpu.SemaphoreType.DMA((13,)),
+            pltpu.SemaphoreType.DMA((14,)),
             pltpu.SemaphoreType.DMA((4,)),
         ],
         compiler_params=pltpu.CompilerParams(
@@ -590,7 +620,7 @@
         out_shape=(out, out),
         in_specs=[anywhere, anywhere],
         out_specs=(anywhere, anywhere),
-        scratch_shapes=[pltpu.SemaphoreType.DMA((8,))],
+        scratch_shapes=[v((4, 128, 512), F32), pltpu.SemaphoreType.DMA((4,)), pltpu.SemaphoreType.DMA((4,))],
         compiler_params=pltpu.CompilerParams(vmem_limit_bytes=56 * 1024 * 1024),
     )(*parts)
 

time: 112 us -> 77.9 us (0.70)
  Pallas kernels: 112 us -> 77.2 us
    pallas_call x1, Pallas kernels: 32.9 us -> 1.98 us  [body(): pl.pallas_call(write_kernel, out_shape=(out, out), in_specs=[anywhere, an...]
    pallas_call x1, Pallas kernels: 78.8 us -> 75.2 us  [body(): pl.pallas_call(kernel, out_shape=(out, out), in_specs=[anywhere, anywhere...]
where the time goes in v3:
time: 77.9 us; the launch traced here: 77.8 us
  Pallas kernels  77.2 us (99%)
    pallas_call x1, Pallas kernels, body(): pl.pallas_call(kernel, out_shape=(out, out), in_specs=[anywhere, anywhere...  75.2 us
    pallas_call x1, Pallas kernels, body(): pl.pallas_call(write_kernel, out_shape=(out, out), in_specs=[anywhere, an...  1.98 us

profile of v3, /device:TPU:1, one launch (start us, length us, event | category | flops | bytes accessed | tf_op | source)
XLA Modules:
  0.0 77.8 jit_solution(15186572994488437218)
XLA Ops:
  0.6 75.2 %shard_map.41 = (f32[256,512]{1,0:T(8,128)}, f32[256,512]{1,0:T(8,128)}) custom-call(f32[256,4096]{1,0:T(8,128)} %first.1, f32[256,4096]{1,0:T(8,128)} %second.1), custom_call_target="tpu_custom_call" | custom-call | tf_op jit(solution)/shard_map/pallas_call | solution.py:568
  75.9 2.0 %shard_map.42 = (f32[256,512]{1,0:T(8,128)}, f32[256,512]{1,0:T(8,128)}) custom-call(f32[256,512]{1,0:T(8,128)} %get-tuple-element.4.a, f32[256,512]{1,0:T(8,128)} %get-tuple-element.5.b), custom_call_target="tpu_custom_call" | custom-call | tf_op jit(solution)/shard_map/pallas_call | solution.py:618

commit v4 on v3

--- a/solution.py
+++ b/solution.py
@@ -21,16 +21,17 @@
 M_Y = 0
 M_ST1 = 12
 M_ST2 = 17
-M_C = 24
-M_ZR = 32
-M_ZG = 48
-M_GD = 64
-M_P1 = 84
-M_P2O = 96
-M_P2R = 100
-M_P2L = 104
-M_X = 108
-M_ALL = 109
+M_ST3 = 24
+M_C = 31
+M_ZR = 39
+M_ZG = 71
+M_GD = 103
+M_P1 = 123
+M_P2O = 135
+M_P2R = 139
+M_P2L = 143
+M_X = 147
+M_ALL = 148
 
 HIGH = lax.Precision.HIGHEST
 
@@ -61,7 +62,7 @@
 
 def kernel(
     first, second, out1, out2,
-    raw, cen, oth, xt, stat, smsg, st1, st2m, st2, fin, scl, fix, nrm, cown, csend, crecv, zs, zr, g,
+    raw, cen, oth, xt, stat, smsg, st1, pst, st2m, st2, fin, dg, scl, fix, nrm, cown, csend, crecv, zs, zr, g,
     acc1, acc2, rsq, csq, rowsq, colsq,
     p1, p1in, p1relay, p2, p2in, p2relay, xs, xr, ob1, ob2, ss, rs, ls, os_,
 ):
@@ -152,13 +153,14 @@
     pl.semaphore_wait(barrier, len(partners))
     y_top = send(M_Y + 0, cen.at[0, top], oth.at[k0, top], sib)
     y_low = send(M_Y + 1, cen.at[1, low], oth.at[k0, low], non)
-    lax.fori_loop(2, 4, local_stats, 0)
     x_in = []
     for n, e in enumerate((1 - iz, iz)):
+        lax.fori_loop(2 + e, 3 + e, local_stats, 0)
+        xt[0, e] = cen[2 + e].T
         x_in.append(
             [
-                send(M_Y + 2 + 2 * n, cen.at[2 + e], oth.at[e], sib),
-                send(M_Y + 3 + 2 * n, cen.at[2 + e], oth.at[4 + e], non),
+                send(M_Y + 2 + 2 * n, xt.at[0, e], xt.at[1, e], sib),
+                send(M_Y + 3 + 2 * n, xt.at[0, e], xt.at[1, 2 + e], non),
             ]
         )
     lax.fori_loop(4, 14, local_stats, 0)
@@ -186,47 +188,40 @@
     y_low.wait_recv()
     l1 = send(M_Y + 8, oth.at[k0, low], oth.at[k1, low], left)
     l3 = send(M_Y + 9, oth.at[k0, low], oth.at[k3, low], right)
-    for a in range(4):
+    for a in range(2, 4):
         xt[0, a] = cen[OWN[AB[a]]].T
     for cp in st_in:
         cp.wait_recv()
 
-    def merge(rows_of, slots, count):
-        devs = []
-        res = []
-        for b in range(8):
-            rows = [rows_of(s, b) for s in range(slots)]
-            total = sum(rows[1:], rows[0])
-            m = total[0:1] * (1.0 / slots)
-            dv = [r[0:1] - m for r in rows]
-            m2 = total[1:2] + count * sum([d * d for d in dv[1:]], dv[0] * dv[0])
-            devs.append(dv)
-            res.append([m, m2, total[2:3], total[3:4]])
-        for b in range(2):
-            cross = sum([p * q for p, q in zip(devs[b][1:], devs[2][1:])], devs[b][0] * devs[2][0])
-            res[b][3] = res[b][3] + count * cross
-        return res
-
-    for b, r in enumerate(merge(lambda s, b: st1[s, b], 4, 256.0)):
-        for n in range(4):
-            st2m[0, b, n : n + 1, :] = r[n]
+    def merge(rows, count):
+        total = sum(rows[1:], rows[0])
+        m = total[0:1] * (1.0 / len(rows))
+        dv = [r[0:1] - m for r in rows]
+        m2 = total[1:2] + count * sum([d * d for d in dv[1:]], dv[0] * dv[0])
+        return m, m2, total[2:3], total[3:4], dv
+
+    def cross(p, q):
+        return sum([a * b for a, b in zip(p[1:], q[1:])], p[0] * q[0])
+
+    merged = [merge([st1[s, b] for s in range(4)], 256.0) for b in range(8)]
+    for b, (m, m2, r, co, dv) in enumerate(merged):
+        if b < 2:
+            co = co + 256.0 * cross(dv, merged[2][4])
+        for n, row in enumerate((m, m2, r, co)):
+            pst[b, n : n + 1, :] = row
+    st2_in = []
     for q in range(8):
         zq = lax.rem(z + q, 8)
         fa = ab(2 * c + lax.div(zq, 4))
         fk = kb(lax.rem(zq, 4))
+        st2m[q, 0] = pst[zq]
+        st2m[q, 3] = pst[2]
+        for s in range(4):
+            st2m[q, 1, s : s + 1, :] = st1[s, fa, 0:1, :]
+            st2m[q, 2, s : s + 1, :] = st1[s, fk, 0:1, :]
         if q:
-            for b in range(8):
-                st2m[q, b] = st2m[0, b]
-        for s in range(4):
-            st2m[q, 8, s : s + 1, :] = st1[s, fa, 0:1, :]
-            st2m[q, 9, s : s + 1, :] = st1[s, fk, 0:1, :]
-    st2_in = [send(M_ST2 + q - 1, st2m.at[q], st2.at[q - 1], zdev[q]) for q in range(1, 8)]
-
-    for n in range(4):
-        acc1[n] = jnp.zeros((512, 256), F32)
-        acc2[n] = jnp.zeros((512, 256), F32)
-    rsq[...] = jnp.zeros_like(rsq)
-    csq[...] = jnp.zeros_like(csq)
+            st2_in.append(send(M_ST2 + q - 1, st2m.at[q], st2.at[q - 1], zdev[q]))
+
     t1.wait_recv()
     yk2 = [send(M_Y + 10, oth.at[k1, top], oth.at[k2, top], left)]
     t3.wait_recv()
@@ -234,10 +229,8 @@
     yk2.append(send(M_Y + 11, oth.at[k3, low], oth.at[k2, low], right))
 
     def x_ready(n):
-        e = (1 - iz, iz)[n]
         for j in range(2):
             x_in[n][j].wait_recv()
-            xt[1, 2 * j + e] = oth[4 * j + e].T
 
     def corr(s, carry):
         r = jnp.where(lax.rem(s, 2) == 1, 4 - lax.div(s + 1, 2), 4 + lax.div(s, 2))
@@ -257,7 +250,7 @@
         make(M_C + s, csend.at[s], crecv.at[s], core).wait_recv()
 
     def zslot(d, t, u):
-        return d * 8 + (t - 1) * 2 + u
+        return d * 16 + (t - 1) * 4 + u * 2
 
     z_in = {}
 
@@ -268,24 +261,36 @@
             c_recv(slot[0])
             if t > 1:
                 c_recv(slot[1])
-        for d in range(2):
-            u = d if far else 1 - d
-            n = slot[d]
-            rows = slice(128 * u, 128 * u + 128)
-            v = cown[n, rows] + crecv[n, rows].astype(F32)
-            if (d, t - 1, u) in z_in:
-                z_in[(d, t - 1, u)].wait_recv()
-                v = v + zr[zslot(d, t - 1, u)].astype(F32)
-            i = zslot(d, t, u)
-            zs[i] = v.astype(BF16)
-            z_in[(d, t, u)] = send(M_ZR + i, zs.at[i], zr.at[i], zto[d])
+        for s in range(2):
+            for d in range(2):
+                u = d if far else 1 - d
+                n = slot[d]
+                rows = slice(128 * u + 64 * s, 128 * u + 64 * s + 64)
+                v = cown[n, rows] + crecv[n, rows].astype(F32)
+                if (d, t - 1, u, s) in z_in:
+                    z_in[(d, t - 1, u, s)].wait_recv()
+                    v = v + zr[zslot(d, t - 1, u) + s].astype(F32)
+                i = zslot(d, t, u) + s
+                zs[i] = v.astype(BF16)
+                z_in[(d, t, u, s)] = send(M_ZR + i, zs.at[i], zr.at[i], zto[d])
 
     x_ready(0)
     lax.fori_loop(0, 1, corr, 0)
+
+    def zero(n, carry):
+        acc1[n] = jnp.zeros((512, 256), F32)
+        acc2[n] = jnp.zeros((512, 256), F32)
+        return carry
+
+    lax.fori_loop(0, 4, zero, 0)
+    rsq[...] = jnp.zeros_like(rsq)
+    csq[...] = jnp.zeros_like(csq)
     x_ready(1)
+    chain(1, True)
     l1.wait_recv()
     lax.fori_loop(1, 3, corr, 0)
-    chain(1, True)
+    for a in range(4):
+        oth[AB[a]] = xt[1, a].T
     chain(2, False)
     for cp in yk2:
         cp.wait_recv()
@@ -296,19 +301,15 @@
 
     for cp in st2_in:
         cp.wait_recv()
-    whole = merge(lambda s, b: st2m[0, b] if s == 0 else st2[s - 1, b], 8, 1024.0)
-    rstds = []
-    for b, r in enumerate(whole):
-        rstd = lax.rsqrt(r[1] * (1.0 / BATCH) + EPS)
-        fin[b, 0:1, :] = r[0] + r[2] * (1.0 / BATCH)
-        fin[b, 1:2, :] = rstd
-        fin[b, 2:3, :] = r[0]
-        fin[b, 3:4, :] = jnp.zeros_like(rstd)
-        rstds.append(rstd)
-    low_half = ylo == 0
-    cii = jnp.where(low_half, whole[0][3] * rstds[0], whole[1][3] * rstds[1]) * rstds[2] * (1.0 / BATCH)
-    fin[8, 0:1, :] = cii
-    fin[8, 1:2, :] = (-2.0 * (1.0 - cii)).astype(BF16).astype(F32)
+    st2m_all = [st2m[0, 0]] + [st2[s, 0] for s in range(7)]
+    k0_means = [st2m[0, 3]] + [st2[s, 3] for s in range(7)]
+    m, m2, r, co, dv = merge(st2m_all, 1024.0)
+    k0_dv = merge(k0_means, 1024.0)[4]
+    fin[z, 0:1, :] = m + r * (1.0 / BATCH)
+    fin[z, 1:2, :] = lax.rsqrt(m2 * (1.0 / BATCH) + EPS)
+    fin[z, 2:3, :] = m
+    fin[z, 3:4, :] = co + 1024.0 * cross(dv, k0_dv)
+    fin_in = [send(M_ST3 + q - 1, fin.at[z], fin.at[z], zdev[q]) for q in range(1, 8)]
 
     def norm(b, carry):
         for src, slot, o in ((None, 0, 0), (oth, 2, 1)):
@@ -329,6 +330,11 @@
         return cen[idx, 128 * h : 128 * h + 128]
 
     chain(3, True)
+    for cp in fin_in:
+        cp.wait_recv()
+    cii = fin[ylo, 3:4, :] * fin[ylo, 1:2, :] * fin[2, 1:2, :] * (1.0 / BATCH)
+    dg[0:1, :] = cii
+    dg[1:2, :] = (-2.0 * (1.0 - cii)).astype(BF16).astype(F32)
     lax.fori_loop(0, 4, norm, 0)
     chain(4, False)
     lax.fori_loop(4, 8, norm, 0)
@@ -342,38 +348,44 @@
     cols_id = lax.broadcasted_iota(jnp.int32, (256, 256), 1)
     off = rows_id + jnp.where((c == 0) & (z == 4 * ylo), 0, 512) != cols_id
     scl[...] = jnp.where(off, tn(ra, rk, HIGH), 0.0)
-    mu_a = [(st2m[0, 8] if s == 0 else st2[s - 1, 8]) - fin[fa, 2:3, :] for s in range(8)]
-    mu_k = [(st2m[0, 9] if s == 0 else st2[s - 1, 9]) - fin[fk, 2:3, :] for s in range(8)]
+    mu_a = [(st2m[0, 1] if s == 0 else st2[s - 1, 1]) - fin[fa, 2:3, :] for s in range(8)]
+    mu_k = [(st2m[0, 2] if s == 0 else st2[s - 1, 2]) - fin[fk, 2:3, :] for s in range(8)]
     fix[...] = scl[...] * tn(jnp.concatenate(mu_a, 0) * 256.0, jnp.concatenate(mu_k, 0), HIGH)
     chain(4, True)
 
     c_recv(7)
-    for u in range(2):
-        rows = slice(128 * u, 128 * u + 128)
-        v = cown[7, rows] + crecv[7, rows].astype(F32)
-        for d in (1 - u, u):
-            z_in[(d, 4, u)].wait_recv()
-            v = v + zr[zslot(d, 4, u)].astype(F32)
-        g[c, z, u] = (v * scl[rows] + fix[rows]).astype(BF16)
-        for d in (u, 1 - u):
-            i = zslot(d, 1, u)
-            send(M_ZG + i, g.at[c, z, u], g.at[c, z, u], zto[d])
-        send(M_GD + u, g.at[c, z, u], g.at[c, z, u], core)
+    for s in range(2):
+        for u in range(2):
+            q = 2 * u + s
+            rows = slice(64 * q, 64 * q + 64)
+            v = cown[7, rows] + crecv[7, rows].astype(F32)
+            for d in (1 - u, u):
+                z_in[(d, 4, u, s)].wait_recv()
+                v = v + zr[zslot(d, 4, u) + s].astype(F32)
+            part = g.at[c, z, q]
+            g[c, z, q] = (v * scl[rows] + fix[rows]).astype(BF16)
+            for d in (u, 1 - u):
+                send(M_ZG + zslot(d, 1, u) + s, part, part, zto[d])
+    send(M_GD + 0, g.at[c, z, pl.ds(0, 2)], g.at[c, z, pl.ds(0, 2)], core)
+    send(M_GD + 1, g.at[c, z, pl.ds(2, 2)], g.at[c, z, pl.ds(2, 2)], core)
 
     def arrive(t, far, onward):
-        for d in range(2):
-            u = d if far else 1 - d
-            i = d * 8 + (t - 1) * 2 + u
-            source = lax.rem(z + (8 - t if d == 0 else t), 8)
-            part = g.at[c, source, u]
-            make(M_ZG + i, part, part, zto[d]).wait_recv()
-            if onward is not None:
-                start = make(M_ZG + i + 2, part, part, zto[d]).start
-                if onward is True:
-                    start()
-                else:
-                    pl.when(onward)(start)
-            make(M_GD + 4 * t + 2 * d + u, part, part, core).start()
+        for s in range(2):
+            for d in range(2):
+                u = d if far else 1 - d
+                i = d * 16 + (t - 1) * 4 + u * 2 + s
+                source = lax.rem(z + (8 - t if d == 0 else t), 8)
+                part = g.at[c, source, 2 * u + s]
+                make(M_ZG + i, part, part, zto[d]).wait_recv()
+                if onward is not None:
+                    start = make(M_ZG + i + 4, part, part, zto[d]).start
+                    if onward is True:
+                        start()
+                    else:
+                        pl.when(onward)(start)
+                if s == 1:
+                    both = g.at[c, source, pl.ds(2 * u, 2)]
+                    make(M_GD + 4 * t + 2 * d + u, both, both, core).start()
 
     def use(j, zs_):
         a = 2 * j + lax.div(zs_, 4)
@@ -387,7 +399,7 @@
         csq[k] += jnp.sum(s.reshape(32, 8, 256), 0)
 
     def from_core(t, d, u):
-        part = g.at[0, 0, 0]
+        part = g.at[0, 0, pl.ds(0, 2)]
         make(M_GD + 4 * t + 2 * d + u, part, part, core).wait_recv()
 
     def uses(t, mine_too):
@@ -414,8 +426,8 @@
         rows = slice(o * 256, o * 256 + 256)
         f = nrm[b, rows].astype(F32)
         v = acc1[a, rows] - f * rowsq[a, 0:1, :]
-        gd = jnp.where(a == ylo, fin[8, 1:2, :], 0.0)
-        v = v + (nrm[2, rows].astype(F32) - f * fin[8, 0:1, :]) * gd
+        gd = jnp.where(a == ylo, dg[1:2, :], 0.0)
+        v = v + (nrm[2, rows].astype(F32) - f * dg[0:1, :]) * gd
         return v * fin[b, 1:2, :]
 
     def p1_start(ph, e):
@@ -465,7 +477,7 @@
         s = nrm[b, rows].astype(F32)
         v = acc2[k, rows] - s * colsq[k]
         if k == 0:
-            v = v + (nrm[ylo, rows].astype(F32) - s * fin[8, 0:1, :]) * fin[8, 1:2, :]
+            v = v + (nrm[ylo, rows].astype(F32) - s * dg[0:1, :]) * dg[1:2, :]
         return v * fin[b, 1:2, :]
 
     def p2_relay(o):
@@ -489,6 +501,24 @@
         p2[3, o, low] = (p2[3, o, low].astype(F32) + p2relay[o, low].astype(F32)).astype(BF16)
         return [a, send(M_P2L + 2 * o + 1, p2.at[3, o, low], p2in.at[1, o, low], left)]
 
+    def sent(i, part):
+        make(i, part, part, core).wait_send()
+
+    def finish_sends():
+        for cp in done:
+            cp.wait_send()
+        for s in range(8):
+            sent(M_C + s, csend.at[s])
+        for d in range(2):
+            for t in range(1, 5):
+                for u in range(2):
+                    if t > 1 and (t < 4 or u == d):
+                        for s in range(2):
+                            sent(M_ZG + zslot(d, t, u) + s, g.at[0, 0, 0])
+                    if t < 4 or u == d:
+                        sent(M_GD + 4 * t + 2 * d + u, g.at[0, 0, pl.ds(0, 2)])
+
+    done = list(sends)
     relay2 = p2_relay(1)
     in1 += p1_add(0, relay1)
     in2 = p2_send(1)
@@ -501,6 +531,7 @@
     ob2[1] = partial2(0, 0)
     in1 += p1_add(1, relay1)
     in20 += p2_add(0, relay20)
+    finish_sends()
     for cp in in2:
         cp.wait_recv()
     xs[...] = (ob2[0] + p2in[0, 1].astype(F32) + p2in[1, 1].astype(F32)).astype(BF16)
@@ -528,37 +559,20 @@
     put(ob2.at[0], out2, hi, 3)
     for cp in outs:
         cp.wait()
-    for cp in sends:
+    for cp in sends[len(done) :]:
         cp.wait_send()
 
-    def sent(i, part):
-        make(i, part, part, core).wait_send()
-
-    for s in range(8):
-        sent(M_C + s, csend.at[s])
-    for d in range(2):
-        for t in range(1, 5):
-            for u in range(2):
-                if t > 1 and (t < 4 or u == d):
-                    sent(M_ZG + zslot(d, t, u), g.at[0, 0, 0])
-                if t < 4 or u == d:
-                    sent(M_GD + 4 * t + 2 * d + u, g.at[0, 0, 0])
-
-
-def write_kernel(a, b, out1, out2, held, sem_in, sem_out):
+
+def write_kernel(a, b, out1, out2, sem):
     cps = []
     for n, (src, dst) in enumerate(((a, out1), (b, out2))):
         for q in range(2):
-            i = 2 * n + q
             rows = pl.ds(128 * q, 128)
-            come = pltpu.make_async_copy(src.at[rows], held.at[i], sem_in.at[i])
-            come.start()
-            cps.append((come, pltpu.make_async_copy(held.at[i], dst.at[rows], sem_out.at[i])))
-    for come, go in cps:
-        come.wait()
-        go.start()
-    for come, go in cps:
-        go.wait()
+            cps.append(pltpu.make_async_copy(src.at[rows], dst.at[rows], sem.at[2 * n + q]))
+    for cp in cps:
+        cp.start()
+    for cp in cps:
+        cp.wait()
 
 
 def body(first, second):
@@ -578,18 +592,20 @@
             v((14, 4, 256), F32),
             v((2, 4, 4, 256), F32),
             v((4, 8, 4, 256), F32),
-            v((8, 10, 4, 256), F32),
-            v((7, 10, 4, 256), F32),
-            v((9, 4, 256), F32),
+            v((8, 4, 256), F32),
+            v((8, 4, 4, 256), F32),
+            v((7, 4, 4, 256), F32),
+            v((8, 4, 256), F32),
+            v((2, 256), F32),
             v((256, 256), F32),
             v((256, 256), F32),
             v((8, 512, 256), BF16),
             v((8, 256, 256), F32),
             v((8, 256, 256), BF16),
             v((8, 256, 256), BF16),
-            v((16, 128, 256), BF16),
-            v((16, 128, 256), BF16),
-            v((2, 8, 2, 128, 256), BF16),
+            v((32, 64, 256), BF16),
+            v((32, 64, 256), BF16),
+            v((2, 8, 4, 64, 256), BF16),
             v((4, 512, 256), F32),
             v((4, 512, 256), F32),
             v((4, 256, 128), F32),
@@ -612,16 +628,16 @@
             pltpu.SemaphoreType.DMA((4,)),
         ],
         compiler_params=pltpu.CompilerParams(
-            collective_id=0, has_side_effects=True, vmem_limit_bytes=56 * 1024 * 1024
+            collective_id=0, has_side_effects=True, vmem_limit_bytes=51 * 1024 * 1024
         ),
     )(first, second)
     return pl.pallas_call(
         write_kernel,
         out_shape=(out, out),
-        in_specs=[anywhere, anywhere],
+        in_specs=[pl.BlockSpec(memory_space=pltpu.VMEM)] * 2,
         out_specs=(anywhere, anywhere),
-        scratch_shapes=[v((4, 128, 512), F32), pltpu.SemaphoreType.DMA((4,)), pltpu.SemaphoreType.DMA((4,))],
-        compiler_params=pltpu.CompilerParams(vmem_limit_bytes=56 * 1024 * 1024),
+        scratch_shapes=[pltpu.SemaphoreType.DMA((4,))],
+        compiler_params=pltpu.CompilerParams(vmem_limit_bytes=8 * 1024 * 1024),
     )(*parts)
 
 

time: 77.9 us -> 72.8 us (0.935)
  Pallas kernels: 77.2 us -> 72.1 us
    pallas_call x1, Pallas kernels: 75.2 us -> 71.1 us  [body(): pl.pallas_call(kernel, out_shape=(out, out), in_specs=[anywhere, anywhere...]
    pallas_call x1, Pallas kernels: 1.98 us -> 1 us  [body(): pl.pallas_call(write_kernel, out_shape=(out, out), in_specs=[pl.BlockSpec...]
where the time goes in v4:
time: 72.8 us; the launch traced here: 72.7 us
  Pallas kernels  72.1 us (99%)
    pallas_call x1, Pallas kernels, body(): pl.pallas_call(kernel, out_shape=(out, out), in_specs=[anywhere, anywhere...  71.1 us

profile of v4, /device:TPU:1, one launch (start us, length us, event | category | flops | bytes accessed | tf_op | source)
XLA Modules:
  0.0 72.7 jit_solution(8352949639850497263)
XLA Ops:
  0.6 71.1 %shard_map.41 = (f32[256,512]{1,0:T(8,128)S(1)}, f32[256,512]{1,0:T(8,128)S(1)}) custom-call(f32[256,4096]{1,0:T(8,128)} %first.1, f32[256,4096]{1,0:T(8,128)} %second.1), custom_call_target="tpu_custom_call" | custom-call | tf_op jit(solution)/shard_map/pallas_call | solution.py:582
  71.7 1.0 %shard_map.42 = (f32[256,512]{1,0:T(8,128)}, f32[256,512]{1,0:T(8,128)}) custom-call(f32[256,512]{1,0:T(8,128)S(1)} %get-tuple-element.4.a, f32[256,512]{1,0:T(8,128)S(1)} %get-tuple-element.5.b), custom_call_target="tpu_custom_call" | custom-call | tf_op jit(solution)/shard_map/pallas_call | solution.py:634

commit v5 on v4

--- a/solution.py
+++ b/solution.py
@@ -86,6 +86,7 @@
     left = dev(lax.rem(x + 3, 4), yhi, ylo, z, c)
     zdev = [dev(x, yhi, ylo, lax.rem(z + q, 8), c) for q in range(8)]
     zto = (zdev[1], zdev[7])
+    zto2 = (zdev[2], zdev[6])
 
     def load(i, ref, col):
         return pltpu.make_async_copy(
@@ -267,12 +268,14 @@
                 n = slot[d]
                 rows = slice(128 * u + 64 * s, 128 * u + 64 * s + 64)
                 v = cown[n, rows] + crecv[n, rows].astype(F32)
-                if (d, t - 1, u, s) in z_in:
-                    z_in[(d, t - 1, u, s)].wait_recv()
-                    v = v + zr[zslot(d, t - 1, u) + s].astype(F32)
+                for before in {2: (), 3: (1, 2), 4: (3,)}.get(t, ()) if far else (t - 1,):
+                    if (d, before, u, s) in z_in:
+                        z_in[(d, before, u, s)].wait_recv()
+                        v = v + zr[zslot(d, before, u) + s].astype(F32)
                 i = zslot(d, t, u) + s
                 zs[i] = v.astype(BF16)
-                z_in[(d, t, u, s)] = send(M_ZR + i, zs.at[i], zr.at[i], zto[d])
+                to = zto2[d] if t == 1 else zto[d]
+                z_in[(d, t, u, s)] = send(M_ZR + i, zs.at[i], zr.at[i], to)
 
     x_ready(0)
     lax.fori_loop(0, 1, corr, 0)
@@ -364,8 +367,9 @@
                 v = v + zr[zslot(d, 4, u) + s].astype(F32)
             part = g.at[c, z, q]
             g[c, z, q] = (v * scl[rows] + fix[rows]).astype(BF16)
-            for d in (u, 1 - u):
-                send(M_ZG + zslot(d, 1, u) + s, part, part, zto[d])
+            send(M_ZG + zslot(u, 1, u) + s, part, part, zto[u])
+            send(M_ZG + zslot(u, 2, u) + s, part, part, zto2[u])
+            send(M_ZG + zslot(1 - u, 1, u) + s, part, part, zto[1 - u])
     send(M_GD + 0, g.at[c, z, pl.ds(0, 2)], g.at[c, z, pl.ds(0, 2)], core)
     send(M_GD + 1, g.at[c, z, pl.ds(2, 2)], g.at[c, z, pl.ds(2, 2)], core)
 
@@ -415,7 +419,7 @@
     uses(0, True)
 
     def step(t, carry):
-        arrive(t, True, True)
+        arrive(t, True, t > 1)
         uses(t - 1, False)
         arrive(t, False, t < 3)
         uses(t, True)
@@ -512,7 +516,7 @@
         for d in range(2):
             for t in range(1, 5):
                 for u in range(2):
-                    if t > 1 and (t < 4 or u == d):
+                    if t > 1 and (t < 4 or u == d) and not (t == 2 and u == d):
                         for s in range(2):
                             sent(M_ZG + zslot(d, t, u) + s, g.at[0, 0, 0])
                     if t < 4 or u == d:

time: 72.8 us -> 73.8 us (1.014)
  Pallas kernels: 72.1 us -> 73 us
    pallas_call x1, Pallas kernels: 71.1 us -> 72 us  [body(): pl.pallas_call(kernel, out_shape=(out, out), in_specs=[anywhere, anywhere...]
where the time goes in v5:
time: 73.8 us; the launch traced here: 73.7 us
  Pallas kernels  73 us (99%)
    pallas_call x1, Pallas kernels, body(): pl.pallas_call(kernel, out_shape=(out, out), in_specs=[anywhere, anywhere...  72 us

profile of v5, /device:TPU:1, one launch (start us, length us, event | category | flops | bytes accessed | tf_op | source)
XLA Modules:
  0.0 73.7 jit_solution(7330708304449539386)
XLA Ops:
  0.6 72.0 %shard_map.41 = (f32[256,512]{1,0:T(8,128)S(1)}, f32[256,512]{1,0:T(8,128)S(1)}) custom-call(f32[256,4096]{1,0:T(8,128)} %first.1, f32[256,4096]{1,0:T(8,128)} %second.1), custom_call_target="tpu_custom_call" | custom-call | tf_op jit(solution)/shard_map/pallas_call | solution.py:586
  72.7 1.0 %shard_map.42 = (f32[256,512]{1,0:T(8,128)}, f32[256,512]{1,0:T(8,128)}) custom-call(f32[256,512]{1,0:T(8,128)S(1)} %get-tuple-element.4.a, f32[256,512]{1,0:T(8,128)S(1)} %get-tuple-element.5.b), custom_call_target="tpu_custom_call" | custom-call | tf_op jit(solution)/shard_map/pallas_call | solution.py:638

commit v6 on v4

--- a/solution.py
+++ b/solution.py
@@ -12,9 +12,9 @@
 BF16 = jnp.bfloat16
 BATCH = 8192
 
-OWN = (2, 3, 10, 11, 8, 9, 12, 13)
-STAT_SIB = (2, 3, 4, 5)
-STAT_NON = (2, 3, 6, 7)
+OWN = (0, 1, 4, 5, 2, 3, 6, 7)
+STAT_SIB = (0, 1, 8, 9)
+STAT_NON = (0, 1, 14, 15)
 KB = (2, 3, 6, 7)
 AB = (0, 1, 4, 5)
 
@@ -23,15 +23,16 @@
 M_ST2 = 17
 M_ST3 = 24
 M_C = 31
-M_ZR = 39
-M_ZG = 71
-M_GD = 103
-M_P1 = 123
-M_P2O = 135
-M_P2R = 139
-M_P2L = 143
-M_X = 147
-M_ALL = 148
+M_YP = 39
+M_ZR = 55
+M_ZG = 87
+M_GD = 119
+M_P1 = 139
+M_P2O = 151
+M_P2R = 155
+M_P2L = 159
+M_X = 163
+M_ALL = 164
 
 HIGH = lax.Precision.HIGHEST
 
@@ -62,7 +63,7 @@
 
 def kernel(
     first, second, out1, out2,
-    raw, cen, oth, xt, stat, smsg, st1, pst, st2m, st2, fin, dg, scl, fix, nrm, cown, csend, crecv, zs, zr, g,
+    raw, cen, oth, xt, stat, smsg, st1, pst, st2m, st2, fin, dg, scl, fix, nrm, cown, ypart, csend, crecv, ys, yr, zs, zr, g,
     acc1, acc2, rsq, csq, rowsq, colsq,
     p1, p1in, p1relay, p2, p2in, p2relay, xs, xr, ob1, ob2, ss, rs, ls, os_,
 ):
@@ -92,27 +93,19 @@
             ref.at[:, pl.ds(pl.multiple_of(col, 256), 256)], raw.at[i], ls.at[i]
         )
 
-    pieces = [lax.rem(x + k, 4) * 512 for k in range(4)]
     kz = lax.rem(z, 4)
     iz = lax.div(z, 4)
-    seed = lax.rem(x + kz, 4) * 512
     base = yhi * 2048
     other = 2048 - base
     mine = x * 512
     lo = ylo * 256
     hi = 256 - lo
-    loads = [
-        load(0, second, base + seed + hi),
-        load(1, second, other + seed + hi),
-        load(2, first, base + mine),
-        load(3, first, base + mine + 256),
-        load(4, second, base + pieces[0] + hi),
-        load(5, second, base + pieces[1] + hi),
-        load(6, second, other + pieces[2] + hi),
-        load(7, second, other + pieces[3] + hi),
-        load(8, first, other + mine),
-        load(9, first, other + mine + 256),
-    ] + [load(10 + k, second, base + pieces[k] + lo) for k in range(4)]
+    loads = [load(2 * j + e, first, (base, other)[j] + mine + 256 * e) for j in range(2) for e in range(2)]
+    for n in range(4):
+        k = lax.rem(kz + n, 4)
+        piece = lax.rem(x + k, 4) * 512
+        for m, col in enumerate((base + lo, base + hi, other + hi)):
+            loads.append(load(4 + 4 * m + k, second, col + piece))
     for cp in loads:
         cp.start()
 
@@ -148,22 +141,52 @@
         return carry
 
     top, low = pl.ds(0, 128), pl.ds(128, 128)
-    k0, k1, k2, k3 = [kb(lax.rem(kz + n, 4)) for n in range(4)]
-    lax.fori_loop(0, 2, local_stats, 0)
+    def blocks_k(m, carry):
+        return local_stats(4 + 4 * lax.rem(m, 3) + lax.rem(kz + lax.div(m, 3), 4), carry)
+
+    lax.fori_loop(0, 4, local_stats, 0)
+
+    def turn(a, carry):
+        xt[a] = cen[a].T
+        return carry
+
+    lax.fori_loop(0, 4, turn, 0)
+    lax.fori_loop(0, 3, blocks_k, 0)
     pl.semaphore_wait(barrier, len(partners))
-    y_top = send(M_Y + 0, cen.at[0, top], oth.at[k0, top], sib)
-    y_low = send(M_Y + 1, cen.at[1, low], oth.at[k0, low], non)
-    x_in = []
-    for n, e in enumerate((1 - iz, iz)):
-        lax.fori_loop(2 + e, 3 + e, local_stats, 0)
-        xt[0, e] = cen[2 + e].T
-        x_in.append(
-            [
-                send(M_Y + 2 + 2 * n, xt.at[0, e], xt.at[1, e], sib),
-                send(M_Y + 3 + 2 * n, xt.at[0, e], xt.at[1, 2 + e], non),
-            ]
+
+    def corr(s, carry):
+        r = jnp.where(lax.rem(s, 2) == 1, 4 - lax.div(s + 1, 2), 4 + lax.div(s, 2))
+        d = lax.rem(z + r, 8)
+        i = lax.div(d, 4)
+        k = lax.rem(d, 4)
+        a = 2 * (1 - c) + i
+        b = 2 * c + i
+        v = nn(jnp.concatenate([xt[a], xt[b]], 0), cen[4 + k])
+        csend[s, 0:256] = v[0:256].astype(BF16)
+        cown[s] = v[256:512]
+        v = nn(jnp.concatenate([xt[a, top], xt[b, top]], 0), cen[8 + k])
+        csend[s, 256:384] = v[0:128].astype(BF16)
+        ypart[s, 0:128] = v[128:256]
+        v = nn(jnp.concatenate([xt[b, low], xt[a, low]], 0), cen[12 + k])
+        csend[s, 384:512] = v[0:128].astype(BF16)
+        ypart[s, 128:256] = v[128:256]
+        make(M_C + s, csend.at[s], crecv.at[s], core).start()
+        return carry
+
+    y_sum = []
+
+    def to_y(s):
+        make(M_C + s, csend.at[s], crecv.at[s], core).wait_recv()
+        ys[s] = (ypart[s] + crecv[s, 256:512].astype(F32)).astype(BF16)
+        y_sum.append(
+            (
+                send(M_YP + 2 * s, ys.at[s, top], yr.at[s, top], sib),
+                send(M_YP + 2 * s + 1, ys.at[s, low], yr.at[s, low], non),
+            )
         )
-    lax.fori_loop(4, 14, local_stats, 0)
+
+    corr(0, 0)
+    lax.fori_loop(3, 12, blocks_k, 0)
 
     def comoment(i, j):
         return jnp.sum((raw[i] - stat[i, 0:1, :]) * (raw[j] - stat[j, 0:1, :]), 0, keepdims=True)
@@ -173,8 +196,8 @@
         smsg[1, n] = stat[STAT_NON[n]]
     for b in range(8):
         st1[0, b] = stat[OWN[b]]
-    smsg[0, 1 - ylo, 3:4, :] = comoment(3 - ylo, 4)
-    st1[0, ylo, 3:4, :] = comoment(2 + ylo, 10)
+    smsg[0, 1 - ylo, 3:4, :] = comoment(1 - ylo, 8)
+    st1[0, ylo, 3:4, :] = comoment(ylo, 4)
     st_in = [
         send(M_ST1 + 0, smsg.at[0], st1.at[2, pl.ds(0, 4)], sib),
         send(M_ST1 + 1, smsg.at[1], st1.at[2, pl.ds(4, 4)], non),
@@ -182,14 +205,10 @@
         send(M_ST1 + 3, smsg.at[1], st1.at[3, pl.ds(4, 4)], nonc),
         send(M_ST1 + 4, st1.at[0], st1.at[1], core),
     ]
-    y_top.wait_recv()
-    t1 = send(M_Y + 6, oth.at[k0, top], oth.at[k1, top], left)
-    t3 = send(M_Y + 7, oth.at[k0, top], oth.at[k3, top], right)
-    y_low.wait_recv()
-    l1 = send(M_Y + 8, oth.at[k0, low], oth.at[k1, low], left)
-    l3 = send(M_Y + 9, oth.at[k0, low], oth.at[k3, low], right)
-    for a in range(2, 4):
-        xt[0, a] = cen[OWN[AB[a]]].T
+    to_y(0)
+    lax.fori_loop(1, 3, corr, 0)
+    to_y(1)
+    to_y(2)
     for cp in st_in:
         cp.wait_recv()
 
@@ -222,32 +241,7 @@
         if q:
             st2_in.append(send(M_ST2 + q - 1, st2m.at[q], st2.at[q - 1], zdev[q]))
 
-    t1.wait_recv()
-    yk2 = [send(M_Y + 10, oth.at[k1, top], oth.at[k2, top], left)]
-    t3.wait_recv()
-    l3.wait_recv()
-    yk2.append(send(M_Y + 11, oth.at[k3, low], oth.at[k2, low], right))
-
-    def x_ready(n):
-        for j in range(2):
-            x_in[n][j].wait_recv()
-
-    def corr(s, carry):
-        r = jnp.where(lax.rem(s, 2) == 1, 4 - lax.div(s + 1, 2), 4 + lax.div(s, 2))
-        d = lax.rem(z + r, 8)
-        i = lax.div(d, 4)
-        k = lax.rem(d, 4)
-        y0 = cen[10 + k]
-        y1 = oth[kb(k)]
-        a = 2 * (1 - c) + i
-        csend[s] = (nn(xt[0, a], y0) + nn(xt[1, a], y1)).astype(BF16)
-        make(M_C + s, csend.at[s], crecv.at[s], core).start()
-        a = 2 * c + i
-        cown[s] = nn(xt[0, a], y0) + nn(xt[1, a], y1)
-        return carry
-
-    def c_recv(s):
-        make(M_C + s, csend.at[s], crecv.at[s], core).wait_recv()
+    lax.fori_loop(3, 5, corr, 0)
 
     def zslot(d, t, u):
         return d * 16 + (t - 1) * 4 + u * 2
@@ -258,15 +252,15 @@
         dist = 5 - t
         slot = (7 - 2 * dist, 8 - 2 * dist) if dist < 4 else (0, 0)
         if (t, far) in ((1, True), (2, False), (3, False), (4, False)):
-            c_recv(slot[0])
-            if t > 1:
-                c_recv(slot[1])
+            for n in set(slot):
+                for cp in y_sum[n]:
+                    cp.wait_recv()
         for s in range(2):
             for d in range(2):
                 u = d if far else 1 - d
                 n = slot[d]
                 rows = slice(128 * u + 64 * s, 128 * u + 64 * s + 64)
-                v = cown[n, rows] + crecv[n, rows].astype(F32)
+                v = cown[n, rows] + crecv[n, rows].astype(F32) + yr[n, rows].astype(F32)
                 if (d, t - 1, u, s) in z_in:
                     z_in[(d, t - 1, u, s)].wait_recv()
                     v = v + zr[zslot(d, t - 1, u) + s].astype(F32)
@@ -274,8 +268,24 @@
                 zs[i] = v.astype(BF16)
                 z_in[(d, t, u, s)] = send(M_ZR + i, zs.at[i], zr.at[i], zto[d])
 
-    x_ready(0)
-    lax.fori_loop(0, 1, corr, 0)
+    chain(1, True)
+    to_y(3)
+    to_y(4)
+    lax.fori_loop(5, 8, corr, 0)
+    chain(2, False)
+    to_y(5)
+    to_y(6)
+    to_y(7)
+
+    x_in = [
+        send(M_Y + 0, cen.at[8, top], oth.at[2, top], sib),
+        send(M_Y + 1, cen.at[12, low], oth.at[2, low], non),
+        send(M_Y + 2, cen.at[0], oth.at[0], sib),
+        send(M_Y + 3, cen.at[0], oth.at[4], non),
+        send(M_Y + 4, cen.at[1], oth.at[1], sib),
+        send(M_Y + 5, cen.at[1], oth.at[5], non),
+    ]
+    chain(2, True)
 
     def zero(n, carry):
         acc1[n] = jnp.zeros((512, 256), F32)
@@ -285,18 +295,6 @@
     lax.fori_loop(0, 4, zero, 0)
     rsq[...] = jnp.zeros_like(rsq)
     csq[...] = jnp.zeros_like(csq)
-    x_ready(1)
-    chain(1, True)
-    l1.wait_recv()
-    lax.fori_loop(1, 3, corr, 0)
-    for a in range(4):
-        oth[AB[a]] = xt[1, a].T
-    chain(2, False)
-    for cp in yk2:
-        cp.wait_recv()
-    lax.fori_loop(3, 5, corr, 0)
-    chain(2, True)
-    lax.fori_loop(5, 8, corr, 0)
     chain(3, False)
 
     for cp in st2_in:
@@ -311,33 +309,38 @@
     fin[z, 3:4, :] = co + 1024.0 * cross(dv, k0_dv)
     fin_in = [send(M_ST3 + q - 1, fin.at[z], fin.at[z], zdev[q]) for q in range(1, 8)]
 
-    def norm(b, carry):
-        for src, slot, o in ((None, 0, 0), (oth, 2, 1)):
-            shift = st1[slot, b, 0:1, :] - fin[b, 0:1, :]
-            scale = fin[b, 1:2, :]
-            for h in range(2):
-                rows = slice(128 * h, 128 * h + 128)
-                v = own_block(b, h) if o == 0 else oth[b, rows]
-                nrm[b, o * 256 + 128 * h : o * 256 + 128 * h + 128, :] = (
-                    (v.astype(F32) + shift) * scale
-                ).astype(BF16)
-        return carry
-
-    def own_block(b, h):
-        p = lax.div(b, 4)
+    chain(3, True)
+    x_in[0].wait_recv()
+    x_in[1].wait_recv()
+    x_ring = [
+        send(M_Y + 6, oth.at[2], oth.at[3], left),
+        send(M_Y + 7, oth.at[2], oth.at[7], right),
+    ]
+    def norm(b, o):
+        shift = st1[2 * o, b, 0:1, :] - fin[b, 0:1, :]
+        scale = fin[b, 1:2, :]
         q = lax.rem(b, 4)
-        idx = jnp.where(q < 2, 2 + q + 6 * p, 8 + q + 2 * p)
-        return cen[idx, 128 * h : 128 * h + 128]
-
-    chain(3, True)
+        idx = jnp.where(q < 2, 0, 2) + q + 2 * lax.div(b, 4)
+        for h in range(2):
+            rows = slice(128 * h, 128 * h + 128)
+            v = cen[idx, rows] if o == 0 else oth[b, rows]
+            nrm[b, o * 256 + 128 * h : o * 256 + 128 * h + 128, :] = ((v.astype(F32) + shift) * scale).astype(BF16)
+
+    def norms(o):
+        lax.fori_loop(0, 8, lambda b, carry: (norm(b, o), carry)[1], 0)
+
+    chain(4, False)
     for cp in fin_in:
         cp.wait_recv()
     cii = fin[ylo, 3:4, :] * fin[ylo, 1:2, :] * fin[2, 1:2, :] * (1.0 / BATCH)
     dg[0:1, :] = cii
     dg[1:2, :] = (-2.0 * (1.0 - cii)).astype(BF16).astype(F32)
-    lax.fori_loop(0, 4, norm, 0)
-    chain(4, False)
-    lax.fori_loop(4, 8, norm, 0)
+    norms(0)
+    chain(4, True)
+    x_ring[0].wait_recv()
+    x_ring.append(send(M_Y + 8, oth.at[3, top], oth.at[6, top], left))
+    x_ring[1].wait_recv()
+    x_ring.append(send(M_Y + 9, oth.at[7, low], oth.at[6, low], right))
 
     fa = ab(2 * c + lax.div(z, 4))
     fk = kb(lax.rem(z, 4))
@@ -351,14 +354,13 @@
     mu_a = [(st2m[0, 1] if s == 0 else st2[s - 1, 1]) - fin[fa, 2:3, :] for s in range(8)]
     mu_k = [(st2m[0, 2] if s == 0 else st2[s - 1, 2]) - fin[fk, 2:3, :] for s in range(8)]
     fix[...] = scl[...] * tn(jnp.concatenate(mu_a, 0) * 256.0, jnp.concatenate(mu_k, 0), HIGH)
-    chain(4, True)
-
-    c_recv(7)
+    for cp in y_sum[7]:
+        cp.wait_recv()
     for s in range(2):
         for u in range(2):
             q = 2 * u + s
             rows = slice(64 * q, 64 * q + 64)
-            v = cown[7, rows] + crecv[7, rows].astype(F32)
+            v = cown[7, rows] + crecv[7, rows].astype(F32) + yr[7, rows].astype(F32)
             for d in (1 - u, u):
                 z_in[(d, 4, u, s)].wait_recv()
                 v = v + zr[zslot(d, 4, u) + s].astype(F32)
@@ -412,6 +414,9 @@
 
         lax.fori_loop(0, jnp.where(t == 0, 1, 2), one, 0)
 
+    for cp in x_in[2:] + x_ring[2:]:
+        cp.wait_recv()
+    norms(1)
     uses(0, True)
 
     def step(t, carry):
@@ -585,11 +590,11 @@
         in_specs=[anywhere, anywhere],
         out_specs=(anywhere, anywhere),
         scratch_shapes=[
-            v((14, 256, 256), F32),
-            v((14, 256, 256), BF16),
+            v((16, 256, 256), F32),
+            v((16, 256, 256), BF16),
             v((8, 256, 256), BF16),
-            v((2, 4, 256, 256), BF16),
-            v((14, 4, 256), F32),
+            v((4, 256, 256), BF16),
+            v((16, 4, 256), F32),
             v((2, 4, 4, 256), F32),
             v((4, 8, 4, 256), F32),
             v((8, 4, 256), F32),
@@ -601,6 +606,9 @@
             v((256, 256), F32),
             v((8, 512, 256), BF16),
             v((8, 256, 256), F32),
+            v((8, 256, 256), F32),
+            v((8, 512, 256), BF16),
+            v((8, 512, 256), BF16),
             v((8, 256, 256), BF16),
             v((8, 256, 256), BF16),
             v((32, 64, 256), BF16),
@@ -624,7 +632,7 @@
             v((2, 256, 256), F32),
             pltpu.SemaphoreType.DMA((M_ALL,)),
             pltpu.SemaphoreType.DMA((M_ALL,)),
-            pltpu.SemaphoreType.DMA((14,)),
+            pltpu.SemaphoreType.DMA((16,)),
             pltpu.SemaphoreType.DMA((4,)),
         ],
         compiler_params=pltpu.CompilerParams(

time: 72.8 us -> 67.5 us (0.927)
  Pallas kernels: 72.1 us -> 66.7 us
    pallas_call x1, Pallas kernels: 71.1 us -> 65.7 us  [body(): pl.pallas_call(kernel, out_shape=(out, out), in_specs=[anywhere, anywhere...]
where the time goes in v6:
time: 67.5 us; the launch traced here: 67.3 us
  Pallas kernels  66.7 us (99%)
    pallas_call x1, Pallas kernels, body(): pl.pallas_call(kernel, out_shape=(out, out), in_specs=[anywhere, anywhere...  65.7 us

profile of v6, /device:TPU:1, one launch (start us, length us, event | category | flops | bytes accessed | tf_op | source)
XLA Modules:
  0.0 67.3 jit_solution(1676644933552663708)
XLA Ops:
  0.6 65.7 %shard_map.41 = (f32[256,512]{1,0:T(8,128)S(1)}, f32[256,512]{1,0:T(8,128)S(1)}) custom-call(f32[256,4096]{1,0:T(8,128)} %first.1, f32[256,4096]{1,0:T(8,128)} %second.1), custom_call_target="tpu_custom_call" | custom-call | tf_op jit(solution)/shard_map/pallas_call | solution.py:587
  66.3 1.0 %shard_map.42 = (f32[256,512]{1,0:T(8,128)}, f32[256,512]{1,0:T(8,128)}) custom-call(f32[256,512]{1,0:T(8,128)S(1)} %get-tuple-element.4.a, f32[256,512]{1,0:T(8,128)S(1)} %get-tuple-element.5.b), custom_call_target="tpu_custom_call" | custom-call | tf_op jit(solution)/shard_map/pallas_call | solution.py:642

commit v7 on v6

--- a/solution.py
+++ b/solution.py
@@ -100,19 +100,24 @@
     mine = x * 512
     lo = ylo * 256
     hi = 256 - lo
-    loads = [load(2 * j + e, first, (base, other)[j] + mine + 256 * e) for j in range(2) for e in range(2)]
-    for n in range(4):
-        k = lax.rem(kz + n, 4)
+    def load_first(e):
+        for j in range(2):
+            load(2 * j + e, first, (base, other)[j] + mine + 256 * e).start()
+
+    def load_second(k):
         piece = lax.rem(x + k, 4) * 512
         for m, col in enumerate((base + lo, base + hi, other + hi)):
-            loads.append(load(4 + 4 * m + k, second, col + piece))
-    for cp in loads:
-        cp.start()
-
+            load(4 + 4 * m + k, second, col + piece).start()
+
+    load_first(1 - iz)
+    load_second(kz)
     barrier = pltpu.get_barrier_semaphore()
     partners = [core, sib, sibc, non, nonc, right, left] + zdev[1:]
     for d in partners:
         pl.semaphore_signal(barrier, inc=1, device_id=d, device_id_type=MESH)
+    load_first(iz)
+    for n in (3, 1, 2):
+        load_second(lax.rem(kz + n, 4))
 
     def make(i, src, dst, to):
         return pltpu.make_async_remote_copy(
@@ -141,16 +146,19 @@
         return carry
 
     top, low = pl.ds(0, 128), pl.ds(128, 128)
+
     def blocks_k(m, carry):
         return local_stats(4 + 4 * lax.rem(m, 3) + lax.rem(kz + lax.div(m, 3), 4), carry)
 
-    lax.fori_loop(0, 4, local_stats, 0)
-
-    def turn(a, carry):
-        xt[a] = cen[a].T
-        return carry
-
-    lax.fori_loop(0, 4, turn, 0)
+    def first_blocks(e):
+        def one(j, carry):
+            local_stats(2 * j + e, carry)
+            xt[2 * j + e] = cen[2 * j + e].T
+            return carry
+
+        lax.fori_loop(0, 2, one, 0)
+
+    first_blocks(1 - iz)
     lax.fori_loop(0, 3, blocks_k, 0)
     pl.semaphore_wait(barrier, len(partners))
 
@@ -186,7 +194,10 @@
         )
 
     corr(0, 0)
+    first_blocks(iz)
     lax.fori_loop(3, 12, blocks_k, 0)
+    to_y(0)
+    lax.fori_loop(1, 3, corr, 0)
 
     def comoment(i, j):
         return jnp.sum((raw[i] - stat[i, 0:1, :]) * (raw[j] - stat[j, 0:1, :]), 0, keepdims=True)
@@ -205,43 +216,8 @@
         send(M_ST1 + 3, smsg.at[1], st1.at[3, pl.ds(4, 4)], nonc),
         send(M_ST1 + 4, st1.at[0], st1.at[1], core),
     ]
-    to_y(0)
-    lax.fori_loop(1, 3, corr, 0)
     to_y(1)
     to_y(2)
-    for cp in st_in:
-        cp.wait_recv()
-
-    def merge(rows, count):
-        total = sum(rows[1:], rows[0])
-        m = total[0:1] * (1.0 / len(rows))
-        dv = [r[0:1] - m for r in rows]
-        m2 = total[1:2] + count * sum([d * d for d in dv[1:]], dv[0] * dv[0])
-        return m, m2, total[2:3], total[3:4], dv
-
-    def cross(p, q):
-        return sum([a * b for a, b in zip(p[1:], q[1:])], p[0] * q[0])
-
-    merged = [merge([st1[s, b] for s in range(4)], 256.0) for b in range(8)]
-    for b, (m, m2, r, co, dv) in enumerate(merged):
-        if b < 2:
-            co = co + 256.0 * cross(dv, merged[2][4])
-        for n, row in enumerate((m, m2, r, co)):
-            pst[b, n : n + 1, :] = row
-    st2_in = []
-    for q in range(8):
-        zq = lax.rem(z + q, 8)
-        fa = ab(2 * c + lax.div(zq, 4))
-        fk = kb(lax.rem(zq, 4))
-        st2m[q, 0] = pst[zq]
-        st2m[q, 3] = pst[2]
-        for s in range(4):
-            st2m[q, 1, s : s + 1, :] = st1[s, fa, 0:1, :]
-            st2m[q, 2, s : s + 1, :] = st1[s, fk, 0:1, :]
-        if q:
-            st2_in.append(send(M_ST2 + q - 1, st2m.at[q], st2.at[q - 1], zdev[q]))
-
-    lax.fori_loop(3, 5, corr, 0)
 
     def zslot(d, t, u):
         return d * 16 + (t - 1) * 4 + u * 2
@@ -269,10 +245,53 @@
                 z_in[(d, t, u, s)] = send(M_ZR + i, zs.at[i], zr.at[i], zto[d])
 
     chain(1, True)
+    lax.fori_loop(3, 5, corr, 0)
+    for cp in st_in:
+        cp.wait_recv()
+
+    def merge(rows, count):
+        total = sum(rows[1:], rows[0])
+        m = total[0:1] * (1.0 / len(rows))
+        dv = [r[0:1] - m for r in rows]
+        m2 = total[1:2] + count * sum([d * d for d in dv[1:]], dv[0] * dv[0])
+        return m, m2, total[2:3], total[3:4], dv
+
+    def cross(p, q):
+        return sum([a * b for a, b in zip(p[1:], q[1:])], p[0] * q[0])
+
+    merged = [merge([st1[s, b] for s in range(4)], 256.0) for b in range(8)]
+    for b, (m, m2, r, co, dv) in enumerate(merged):
+        if b < 2:
+            co = co + 256.0 * cross(dv, merged[2][4])
+        for n, row in enumerate((m, m2, r, co)):
+            pst[b, n : n + 1, :] = row
+    st2_in = []
+    for q in range(8):
+        zq = lax.rem(z + q, 8)
+        fa = ab(2 * c + lax.div(zq, 4))
+        fk = kb(lax.rem(zq, 4))
+        st2m[q, 0] = pst[zq]
+        st2m[q, 3] = pst[2]
+        for s in range(4):
+            st2m[q, 1, s : s + 1, :] = st1[s, fa, 0:1, :]
+            st2m[q, 2, s : s + 1, :] = st1[s, fk, 0:1, :]
+        if q:
+            st2_in.append(send(M_ST2 + q - 1, st2m.at[q], st2.at[q - 1], zdev[q]))
+
     to_y(3)
     to_y(4)
+    chain(2, False)
+    chain(2, True)
     lax.fori_loop(5, 8, corr, 0)
-    chain(2, False)
+
+    def zero(n, carry):
+        acc1[n] = jnp.zeros((512, 256), F32)
+        acc2[n] = jnp.zeros((512, 256), F32)
+        return carry
+
+    lax.fori_loop(0, 4, zero, 0)
+    rsq[...] = jnp.zeros_like(rsq)
+    csq[...] = jnp.zeros_like(csq)
     to_y(5)
     to_y(6)
     to_y(7)
@@ -285,16 +304,6 @@
         send(M_Y + 4, cen.at[1], oth.at[1], sib),
         send(M_Y + 5, cen.at[1], oth.at[5], non),
     ]
-    chain(2, True)
-
-    def zero(n, carry):
-        acc1[n] = jnp.zeros((512, 256), F32)
-        acc2[n] = jnp.zeros((512, 256), F32)
-        return carry
-
-    lax.fori_loop(0, 4, zero, 0)
-    rsq[...] = jnp.zeros_like(rsq)
-    csq[...] = jnp.zeros_like(csq)
     chain(3, False)
 
     for cp in st2_in:
@@ -316,6 +325,7 @@
         send(M_Y + 6, oth.at[2], oth.at[3], left),
         send(M_Y + 7, oth.at[2], oth.at[7], right),
     ]
+
     def norm(b, o):
         shift = st1[2 * o, b, 0:1, :] - fin[b, 0:1, :]
         scale = fin[b, 1:2, :]
@@ -354,6 +364,7 @@
     mu_a = [(st2m[0, 1] if s == 0 else st2[s - 1, 1]) - fin[fa, 2:3, :] for s in range(8)]
     mu_k = [(st2m[0, 2] if s == 0 else st2[s - 1, 2]) - fin[fk, 2:3, :] for s in range(8)]
     fix[...] = scl[...] * tn(jnp.concatenate(mu_a, 0) * 256.0, jnp.concatenate(mu_k, 0), HIGH)
+
     for cp in y_sum[7]:
         cp.wait_recv()
     for s in range(2):

time: 67.5 us -> 71.3 us (1.056)
  Pallas kernels: 66.7 us -> 69.9 us
    pallas_call x1, Pallas kernels: 65.7 us -> 68.9 us  [body(): pl.pallas_call(kernel, out_shape=(out, out), in_specs=[anywhere, anywhere...]
where the time goes in v7:
time: 71.3 us; the launch traced here: 70.5 us
  Pallas kernels  69.9 us (98%)
    pallas_call x1, Pallas kernels, body(): pl.pallas_call(kernel, out_shape=(out, out), in_specs=[anywhere, anywhere...  68.9 us

profile of v7, /device:TPU:1, one launch (start us, length us, event | category | flops | bytes accessed | tf_op | source)
XLA Modules:
  0.0 70.5 jit_solution(2601673951552113360)
XLA Ops:
  0.6 68.9 %shard_map.41 = (f32[256,512]{1,0:T(8,128)S(1)}, f32[256,512]{1,0:T(8,128)S(1)}) custom-call(f32[256,4096]{1,0:T(8,128)} %first.1, f32[256,4096]{1,0:T(8,128)} %second.1), custom_call_target="tpu_custom_call" | custom-call | tf_op jit(solution)/shard_map/pallas_call | solution.py:598
  69.5 1.0 %shard_map.42 = (f32[256,512]{1,0:T(8,128)}, f32[256,512]{1,0:T(8,128)}) custom-call(f32[256,512]{1,0:T(8,128)S(1)} %get-tuple-element.4.a, f32[256,512]{1,0:T(8,128)S(1)} %get-tuple-element.5.b), custom_call_target="tpu_custom_call" | custom-call | tf_op jit(solution)/shard_map/pallas_call | solution.py:653

commit v8 on v7

--- a/solution.py
+++ b/solution.py
@@ -196,29 +196,6 @@
     corr(0, 0)
     first_blocks(iz)
     lax.fori_loop(3, 12, blocks_k, 0)
-    to_y(0)
-    lax.fori_loop(1, 3, corr, 0)
-
-    def comoment(i, j):
-        return jnp.sum((raw[i] - stat[i, 0:1, :]) * (raw[j] - stat[j, 0:1, :]), 0, keepdims=True)
-
-    for n in range(4):
-        smsg[0, n] = stat[STAT_SIB[n]]
-        smsg[1, n] = stat[STAT_NON[n]]
-    for b in range(8):
-        st1[0, b] = stat[OWN[b]]
-    smsg[0, 1 - ylo, 3:4, :] = comoment(1 - ylo, 8)
-    st1[0, ylo, 3:4, :] = comoment(ylo, 4)
-    st_in = [
-        send(M_ST1 + 0, smsg.at[0], st1.at[2, pl.ds(0, 4)], sib),
-        send(M_ST1 + 1, smsg.at[1], st1.at[2, pl.ds(4, 4)], non),
-        send(M_ST1 + 2, smsg.at[0], st1.at[3, pl.ds(0, 4)], sibc),
-        send(M_ST1 + 3, smsg.at[1], st1.at[3, pl.ds(4, 4)], nonc),
-        send(M_ST1 + 4, st1.at[0], st1.at[1], core),
-    ]
-    to_y(1)
-    to_y(2)
-
     def zslot(d, t, u):
         return d * 16 + (t - 1) * 4 + u * 2
 
@@ -244,8 +221,37 @@
                 zs[i] = v.astype(BF16)
                 z_in[(d, t, u, s)] = send(M_ZR + i, zs.at[i], zr.at[i], zto[d])
 
+    to_y(0)
+    lax.fori_loop(1, 5, corr, 0)
+    to_y(1)
+    to_y(2)
     chain(1, True)
-    lax.fori_loop(3, 5, corr, 0)
+    to_y(3)
+    to_y(4)
+
+    def comoment(i, j):
+        return jnp.sum((raw[i] - stat[i, 0:1, :]) * (raw[j] - stat[j, 0:1, :]), 0, keepdims=True)
+
+    for n in range(4):
+        smsg[0, n] = stat[STAT_SIB[n]]
+        smsg[1, n] = stat[STAT_NON[n]]
+    for b in range(8):
+        st1[0, b] = stat[OWN[b]]
+    smsg[0, 1 - ylo, 3:4, :] = comoment(1 - ylo, 8)
+    st1[0, ylo, 3:4, :] = comoment(ylo, 4)
+    st_in = [
+        send(M_ST1 + 0, smsg.at[0], st1.at[2, pl.ds(0, 4)], sib),
+        send(M_ST1 + 1, smsg.at[1], st1.at[2, pl.ds(4, 4)], non),
+        send(M_ST1 + 2, smsg.at[0], st1.at[3, pl.ds(0, 4)], sibc),
+        send(M_ST1 + 3, smsg.at[1], st1.at[3, pl.ds(4, 4)], nonc),
+        send(M_ST1 + 4, st1.at[0], st1.at[1], core),
+    ]
+    lax.fori_loop(5, 8, corr, 0)
+    chain(2, False)
+    to_y(5)
+    to_y(6)
+    chain(2, True)
+    to_y(7)
     for cp in st_in:
         cp.wait_recv()
 
@@ -278,24 +284,6 @@
         if q:
             st2_in.append(send(M_ST2 + q - 1, st2m.at[q], st2.at[q - 1], zdev[q]))
 
-    to_y(3)
-    to_y(4)
-    chain(2, False)
-    chain(2, True)
-    lax.fori_loop(5, 8, corr, 0)
-
-    def zero(n, carry):
-        acc1[n] = jnp.zeros((512, 256), F32)
-        acc2[n] = jnp.zeros((512, 256), F32)
-        return carry
-
-    lax.fori_loop(0, 4, zero, 0)
-    rsq[...] = jnp.zeros_like(rsq)
-    csq[...] = jnp.zeros_like(csq)
-    to_y(5)
-    to_y(6)
-    to_y(7)
-
     x_in = [
         send(M_Y + 0, cen.at[8, top], oth.at[2, top], sib),
         send(M_Y + 1, cen.at[12, low], oth.at[2, low], non),
@@ -304,6 +292,15 @@
         send(M_Y + 4, cen.at[1], oth.at[1], sib),
         send(M_Y + 5, cen.at[1], oth.at[5], non),
     ]
+
+    def zero(n, carry):
+        acc1[n] = jnp.zeros((512, 256), F32)
+        acc2[n] = jnp.zeros((512, 256), F32)
+        return carry
+
+    lax.fori_loop(0, 4, zero, 0)
+    rsq[...] = jnp.zeros_like(rsq)
+    csq[...] = jnp.zeros_like(csq)
     chain(3, False)
 
     for cp in st2_in:

time: 71.3 us -> 72.1 us (1.011)
  Pallas kernels: 69.9 us -> 71.3 us
    pallas_call x1, Pallas kernels: 68.9 us -> 70.3 us  [body(): pl.pallas_call(kernel, out_shape=(out, out), in_specs=[anywhere, anywhere...]
where the time goes in v8:
time: 72.1 us; the launch traced here: 72 us
  Pallas kernels  71.3 us (99%)
    pallas_call x1, Pallas kernels, body(): pl.pallas_call(kernel, out_shape=(out, out), in_specs=[anywhere, anywhere...  70.3 us

profile of v8, /device:TPU:1, one launch (start us, length us, event | category | flops | bytes accessed | tf_op | source)
XLA Modules:
  0.0 72.0 jit_solution(12570287747871106201)
XLA Ops:
  0.6 70.3 %shard_map.41 = (f32[256,512]{1,0:T(8,128)S(1)}, f32[256,512]{1,0:T(8,128)S(1)}) custom-call(f32[256,4096]{1,0:T(8,128)} %first.1, f32[256,4096]{1,0:T(8,128)} %second.1), custom_call_target="tpu_custom_call" | custom-call | tf_op jit(solution)/shard_map/pallas_call | solution.py:595
  71.0 1.0 %shard_map.42 = (f32[256,512]{1,0:T(8,128)}, f32[256,512]{1,0:T(8,128)}) custom-call(f32[256,512]{1,0:T(8,128)S(1)} %get-tuple-element.4.a, f32[256,512]{1,0:T(8,128)S(1)} %get-tuple-element.5.b), custom_call_target="tpu_custom_call" | custom-call | tf_op jit(solution)/shard_map/pallas_call | solution.py:650

commit v9 on v8

--- a/solution.py
+++ b/solution.py
@@ -221,14 +221,6 @@
                 zs[i] = v.astype(BF16)
                 z_in[(d, t, u, s)] = send(M_ZR + i, zs.at[i], zr.at[i], zto[d])
 
-    to_y(0)
-    lax.fori_loop(1, 5, corr, 0)
-    to_y(1)
-    to_y(2)
-    chain(1, True)
-    to_y(3)
-    to_y(4)
-
     def comoment(i, j):
         return jnp.sum((raw[i] - stat[i, 0:1, :]) * (raw[j] - stat[j, 0:1, :]), 0, keepdims=True)
 
@@ -246,12 +238,10 @@
         send(M_ST1 + 3, smsg.at[1], st1.at[3, pl.ds(4, 4)], nonc),
         send(M_ST1 + 4, st1.at[0], st1.at[1], core),
     ]
-    lax.fori_loop(5, 8, corr, 0)
-    chain(2, False)
-    to_y(5)
-    to_y(6)
-    chain(2, True)
-    to_y(7)
+    to_y(0)
+    lax.fori_loop(1, 5, corr, 0)
+    to_y(1)
+    to_y(2)
     for cp in st_in:
         cp.wait_recv()
 
@@ -284,25 +274,11 @@
         if q:
             st2_in.append(send(M_ST2 + q - 1, st2m.at[q], st2.at[q - 1], zdev[q]))
 
-    x_in = [
-        send(M_Y + 0, cen.at[8, top], oth.at[2, top], sib),
-        send(M_Y + 1, cen.at[12, low], oth.at[2, low], non),
-        send(M_Y + 2, cen.at[0], oth.at[0], sib),
-        send(M_Y + 3, cen.at[0], oth.at[4], non),
-        send(M_Y + 4, cen.at[1], oth.at[1], sib),
-        send(M_Y + 5, cen.at[1], oth.at[5], non),
-    ]
-
-    def zero(n, carry):
-        acc1[n] = jnp.zeros((512, 256), F32)
-        acc2[n] = jnp.zeros((512, 256), F32)
-        return carry
-
-    lax.fori_loop(0, 4, zero, 0)
-    rsq[...] = jnp.zeros_like(rsq)
-    csq[...] = jnp.zeros_like(csq)
-    chain(3, False)
-
+    to_y(3)
+    to_y(4)
+    chain(1, True)
+
+    lax.fori_loop(5, 8, corr, 0)
     for cp in st2_in:
         cp.wait_recv()
     st2m_all = [st2m[0, 0]] + [st2[s, 0] for s in range(7)]
@@ -314,6 +290,30 @@
     fin[z, 2:3, :] = m
     fin[z, 3:4, :] = co + 1024.0 * cross(dv, k0_dv)
     fin_in = [send(M_ST3 + q - 1, fin.at[z], fin.at[z], zdev[q]) for q in range(1, 8)]
+
+    to_y(5)
+    to_y(6)
+    to_y(7)
+    chain(2, False)
+    x_in = [
+        send(M_Y + 0, cen.at[8, top], oth.at[2, top], sib),
+        send(M_Y + 1, cen.at[12, low], oth.at[2, low], non),
+        send(M_Y + 2, cen.at[0], oth.at[0], sib),
+        send(M_Y + 3, cen.at[0], oth.at[4], non),
+        send(M_Y + 4, cen.at[1], oth.at[1], sib),
+        send(M_Y + 5, cen.at[1], oth.at[5], non),
+    ]
+    chain(2, True)
+
+    def zero(n, carry):
+        acc1[n] = jnp.zeros((512, 256), F32)
+        acc2[n] = jnp.zeros((512, 256), F32)
+        return carry
+
+    lax.fori_loop(0, 4, zero, 0)
+    rsq[...] = jnp.zeros_like(rsq)
+    csq[...] = jnp.zeros_like(csq)
+    chain(3, False)
 
     chain(3, True)
     x_in[0].wait_recv()

time: 72.1 us -> 69.1 us (0.958)
  Pallas kernels: 71.3 us -> 67.9 us
    pallas_call x1, Pallas kernels: 70.3 us -> 66.9 us  [body(): pl.pallas_call(kernel, out_shape=(out, out), in_specs=[anywhere, anywhere...]
where the time goes in v9:
time: 69.1 us; the launch traced here: 68.6 us
  Pallas kernels  67.9 us (98%)
    pallas_call x1, Pallas kernels, body(): pl.pallas_call(kernel, out_shape=(out, out), in_specs=[anywhere, anywhere...  66.9 us

profile of v9, /device:TPU:1, one launch (start us, length us, event | category | flops | bytes accessed | tf_op | source)
XLA Modules:
  0.0 68.6 jit_solution(16039801022321662460)
XLA Ops:
  0.6 66.9 %shard_map.41 = (f32[256,512]{1,0:T(8,128)S(1)}, f32[256,512]{1,0:T(8,128)S(1)}) custom-call(f32[256,4096]{1,0:T(8,128)} %first.1, f32[256,4096]{1,0:T(8,128)} %second.1), custom_call_target="tpu_custom_call" | custom-call | tf_op jit(solution)/shard_map/pallas_call | solution.py:595
  67.6 1.0 %shard_map.42 = (f32[256,512]{1,0:T(8,128)}, f32[256,512]{1,0:T(8,128)}) custom-call(f32[256,512]{1,0:T(8,128)S(1)} %get-tuple-element.4.a, f32[256,512]{1,0:T(8,128)S(1)} %get-tuple-element.5.b), custom_call_target="tpu_custom_call" | custom-call | tf_op jit(solution)/shard_map/pallas_call | solution.py:650

commit v10 on v9

--- a/solution.py
+++ b/solution.py
@@ -279,6 +279,28 @@
     chain(1, True)
 
     lax.fori_loop(5, 8, corr, 0)
+    chain(2, False)
+    to_y(5)
+    to_y(6)
+    to_y(7)
+    x_in = [
+        send(M_Y + 0, cen.at[8, top], oth.at[2, top], sib),
+        send(M_Y + 1, cen.at[12, low], oth.at[2, low], non),
+        send(M_Y + 2, cen.at[0], oth.at[0], sib),
+        send(M_Y + 3, cen.at[0], oth.at[4], non),
+        send(M_Y + 4, cen.at[1], oth.at[1], sib),
+        send(M_Y + 5, cen.at[1], oth.at[5], non),
+    ]
+    chain(2, True)
+
+    def zero(n, carry):
+        acc1[n] = jnp.zeros((512, 256), F32)
+        acc2[n] = jnp.zeros((512, 256), F32)
+        return carry
+
+    lax.fori_loop(0, 4, zero, 0)
+    rsq[...] = jnp.zeros_like(rsq)
+    csq[...] = jnp.zeros_like(csq)
     for cp in st2_in:
         cp.wait_recv()
     st2m_all = [st2m[0, 0]] + [st2[s, 0] for s in range(7)]
@@ -291,28 +313,6 @@
     fin[z, 3:4, :] = co + 1024.0 * cross(dv, k0_dv)
     fin_in = [send(M_ST3 + q - 1, fin.at[z], fin.at[z], zdev[q]) for q in range(1, 8)]
 
-    to_y(5)
-    to_y(6)
-    to_y(7)
-    chain(2, False)
-    x_in = [
-        send(M_Y + 0, cen.at[8, top], oth.at[2, top], sib),
-        send(M_Y + 1, cen.at[12, low], oth.at[2, low], non),
-        send(M_Y + 2, cen.at[0], oth.at[0], sib),
-        send(M_Y + 3, cen.at[0], oth.at[4], non),
-        send(M_Y + 4, cen.at[1], oth.at[1], sib),
-        send(M_Y + 5, cen.at[1], oth.at[5], non),
-    ]
-    chain(2, True)
-
-    def zero(n, carry):
-        acc1[n] = jnp.zeros((512, 256), F32)
-        acc2[n] = jnp.zeros((512, 256), F32)
-        return carry
-
-    lax.fori_loop(0, 4, zero, 0)
-    rsq[...] = jnp.zeros_like(rsq)
-    csq[...] = jnp.zeros_like(csq)
     chain(3, False)
 
     chain(3, True)

time: 69.1 us -> 67.6 us (0.978)
  Pallas kernels: 67.9 us -> 66.6 us
    pallas_call x1, Pallas kernels: 66.9 us -> 65.6 us  [body(): pl.pallas_call(kernel, out_shape=(out, out), in_specs=[anywhere, anywhere...]
where the time goes in v10:
time: 67.6 us; the launch traced here: 67.3 us
  Pallas kernels  66.6 us (99%)
    pallas_call x1, Pallas kernels, body(): pl.pallas_call(kernel, out_shape=(out, out), in_specs=[anywhere, anywhere...  65.6 us

profile of v10, /device:TPU:1, one launch (start us, length us, event | category | flops | bytes accessed | tf_op | source)
XLA Modules:
  0.0 67.3 jit_solution(10589108370108336396)
XLA Ops:
  0.6 65.6 %shard_map.41 = (f32[256,512]{1,0:T(8,128)S(1)}, f32[256,512]{1,0:T(8,128)S(1)}) custom-call(f32[256,4096]{1,0:T(8,128)} %first.1, f32[256,4096]{1,0:T(8,128)} %second.1), custom_call_target="tpu_custom_call" | custom-call | tf_op jit(solution)/shard_map/pallas_call | solution.py:595
  66.3 1.0 %shard_map.42 = (f32[256,512]{1,0:T(8,128)}, f32[256,512]{1,0:T(8,128)}) custom-call(f32[256,512]{1,0:T(8,128)S(1)} %get-tuple-element.4.a, f32[256,512]{1,0:T(8,128)S(1)} %get-tuple-element.5.b), custom_call_target="tpu_custom_call" | custom-call | tf_op jit(solution)/shard_map/pallas_call | solution.py:650

commit v11 on v10

--- a/solution.py
+++ b/solution.py
@@ -276,6 +276,10 @@
 
     to_y(3)
     to_y(4)
+    x_in = [
+        send(M_Y + 0, cen.at[8, top], oth.at[2, top], sib),
+        send(M_Y + 1, cen.at[12, low], oth.at[2, low], non),
+    ]
     chain(1, True)
 
     lax.fori_loop(5, 8, corr, 0)
@@ -283,9 +287,7 @@
     to_y(5)
     to_y(6)
     to_y(7)
-    x_in = [
-        send(M_Y + 0, cen.at[8, top], oth.at[2, top], sib),
-        send(M_Y + 1, cen.at[12, low], oth.at[2, low], non),
+    x_in += [
         send(M_Y + 2, cen.at[0], oth.at[0], sib),
         send(M_Y + 3, cen.at[0], oth.at[4], non),
         send(M_Y + 4, cen.at[1], oth.at[1], sib),
@@ -301,6 +303,12 @@
     lax.fori_loop(0, 4, zero, 0)
     rsq[...] = jnp.zeros_like(rsq)
     csq[...] = jnp.zeros_like(csq)
+    x_in[0].wait_recv()
+    x_in[1].wait_recv()
+    x_ring = [
+        send(M_Y + 6, oth.at[2], oth.at[3], left),
+        send(M_Y + 7, oth.at[2], oth.at[7], right),
+    ]
     for cp in st2_in:
         cp.wait_recv()
     st2m_all = [st2m[0, 0]] + [st2[s, 0] for s in range(7)]
@@ -316,12 +324,6 @@
     chain(3, False)
 
     chain(3, True)
-    x_in[0].wait_recv()
-    x_in[1].wait_recv()
-    x_ring = [
-        send(M_Y + 6, oth.at[2], oth.at[3], left),
-        send(M_Y + 7, oth.at[2], oth.at[7], right),
-    ]
 
     def norm(b, o):
         shift = st1[2 * o, b, 0:1, :] - fin[b, 0:1, :]
@@ -336,6 +338,10 @@
     def norms(o):
         lax.fori_loop(0, 8, lambda b, carry: (norm(b, o), carry)[1], 0)
 
+    x_ring[0].wait_recv()
+    x_ring.append(send(M_Y + 8, oth.at[3, top], oth.at[6, top], left))
+    x_ring[1].wait_recv()
+    x_ring.append(send(M_Y + 9, oth.at[7, low], oth.at[6, low], right))
     chain(4, False)
     for cp in fin_in:
         cp.wait_recv()
@@ -344,10 +350,6 @@
     dg[1:2, :] = (-2.0 * (1.0 - cii)).astype(BF16).astype(F32)
     norms(0)
     chain(4, True)
-    x_ring[0].wait_recv()
-    x_ring.append(send(M_Y + 8, oth.at[3, top], oth.at[6, top], left))
-    x_ring[1].wait_recv()
-    x_ring.append(send(M_Y + 9, oth.at[7, low], oth.at[6, low], right))
 
     fa = ab(2 * c + lax.div(z, 4))
     fk = kb(lax.rem(z, 4))
@@ -422,10 +424,14 @@
 
         lax.fori_loop(0, jnp.where(t == 0, 1, 2), one, 0)
 
+    arrive(1, True, True)
+    arrive(1, False, True)
     for cp in x_in[2:] + x_ring[2:]:
         cp.wait_recv()
     norms(1)
     uses(0, True)
+    uses(0, False)
+    uses(1, True)
 
     def step(t, carry):
         arrive(t, True, True)
@@ -467,7 +473,7 @@
         p1[ph, 2, low] = (p1[ph, 2, low].astype(F32) + p1relay[ph, low].astype(F32)).astype(BF16)
         return [a, send(m + 5, p1.at[ph, 2, low], p1in.at[ph, 0, low], sib)]
 
-    lax.fori_loop(1, 4, step, 0)
+    lax.fori_loop(2, 4, step, 0)
     uses(3, False)
     relay1, in1 = p1_start(0, iz)
     arrive(4, True, None)

time: 67.6 us -> 67 us (level)
  no operation moved by 1% of the time
where the time goes in v11:
time: 67 us; the launch traced here: 66.7 us
  Pallas kernels  66 us (99%)
    pallas_call x1, Pallas kernels, body(): pl.pallas_call(kernel, out_shape=(out, out), in_specs=[anywhere, anywhere...  65 us

profile of v11, /device:TPU:1, one launch (start us, length us, event | category | flops | bytes accessed | tf_op | source)
XLA Modules:
  0.0 66.7 jit_solution(332655201482805436)
XLA Ops:
  0.6 65.0 %shard_map.41 = (f32[256,512]{1,0:T(8,128)S(1)}, f32[256,512]{1,0:T(8,128)S(1)}) custom-call(f32[256,4096]{1,0:T(8,128)} %first.1, f32[256,4096]{1,0:T(8,128)} %second.1), custom_call_target="tpu_custom_call" | custom-call | tf_op jit(solution)/shard_map/pallas_call | solution.py:601
  65.7 1.0 %shard_map.42 = (f32[256,512]{1,0:T(8,128)}, f32[256,512]{1,0:T(8,128)}) custom-call(f32[256,512]{1,0:T(8,128)S(1)} %get-tuple-element.4.a, f32[256,512]{1,0:T(8,128)S(1)} %get-tuple-element.5.b), custom_call_target="tpu_custom_call" | custom-call | tf_op jit(solution)/shard_map/pallas_call | solution.py:656

commit v12 on v11

--- a/solution.py
+++ b/solution.py
@@ -399,45 +399,42 @@
                     both = g.at[c, source, pl.ds(2 * u, 2)]
                     make(M_GD + 4 * t + 2 * d + u, both, both, core).start()
 
-    def use(j, zs_):
-        a = 2 * j + lax.div(zs_, 4)
+    def use(zs_):
+        i = lax.div(zs_, 4)
         k = lax.rem(zs_, 4)
-        ga = g[j, zs_].reshape(256, 256)
-        acc1[a] += nt(nrm[kb(k)], ga)
-        acc2[k] += nn(nrm[ab(a)], ga)
+        ga = jnp.concatenate([g[0, zs_].reshape(256, 256), g[1, zs_].reshape(256, 256)], 0)
+        v = nt(nrm[kb(k)], ga)
+        acc1[i] += v[:, 0:256]
+        acc1[2 + i] += v[:, 256:512]
+        acc2[k] += nn(jnp.concatenate([nrm[i], nrm[4 + i]], 1), ga)
         v = ga.astype(F32)
         s = v * v
-        rsq[a] += s[:, 0:128] + s[:, 128:256]
-        csq[k] += jnp.sum(s.reshape(32, 8, 256), 0)
+        part = s[:, 0:128] + s[:, 128:256]
+        rsq[i] += part[0:256]
+        rsq[2 + i] += part[256:512]
+        csq[k] += jnp.sum(s.reshape(64, 8, 256), 0)
 
     def from_core(t, d, u):
         part = g.at[0, 0, pl.ds(0, 2)]
         make(M_GD + 4 * t + 2 * d + u, part, part, core).wait_recv()
 
-    def uses(t, mine_too):
-        def one(n, inner):
-            if not mine_too:
-                for u in range(2):
-                    from_core(t, n, u)
-            use(c if mine_too else 1 - c, lax.rem(z + (8 - t) + n * 2 * t, 8))
-            return inner
-
-        lax.fori_loop(0, jnp.where(t == 0, 1, 2), one, 0)
+    def uses(t, n):
+        for u in range(2):
+            from_core(t, n, u)
+        use(lax.rem(z + (8 - t) + n * 2 * t, 8))
 
     arrive(1, True, True)
     arrive(1, False, True)
     for cp in x_in[2:] + x_ring[2:]:
         cp.wait_recv()
     norms(1)
-    uses(0, True)
-    uses(0, False)
-    uses(1, True)
+    uses(0, 0)
 
     def step(t, carry):
         arrive(t, True, True)
-        uses(t - 1, False)
+        uses(t - 1, 0)
         arrive(t, False, t < 3)
-        uses(t, True)
+        uses(t - 1, 1)
         return carry
 
     def partial1(a, o):
@@ -474,18 +471,12 @@
         return [a, send(m + 5, p1.at[ph, 2, low], p1in.at[ph, 0, low], sib)]
 
     lax.fori_loop(2, 4, step, 0)
-    uses(3, False)
+    lax.fori_loop(0, 2, lambda n, carry: (uses(3, n), carry)[1], 0)
     relay1, in1 = p1_start(0, iz)
     arrive(4, True, None)
-
-    def final_two(n, carry):
-        use(lax.rem(c + n, 2), lax.rem(z + 4, 8))
-        return carry
-
-    lax.fori_loop(0, 1, final_two, 0)
     from_core(4, 0, 0)
     from_core(4, 1, 1)
-    lax.fori_loop(1, 2, final_two, 0)
+    use(lax.rem(z + 4, 8))
 
     for k in range(4):
         colsq[k] = jnp.sum(csq[k], 0, keepdims=True) * (0.5 / LAMBDA)

time: 67 us -> 67 us (level)
  no operation moved by 1% of the time
where the time goes in v12:
time: 67 us; the launch traced here: 66.6 us
  Pallas kernels  66 us (99%)
    pallas_call x1, Pallas kernels, body(): pl.pallas_call(kernel, out_shape=(out, out), in_specs=[anywhere, anywhere...  65 us

profile of v12, /device:TPU:1, one launch (start us, length us, event | category | flops | bytes accessed | tf_op | source)
XLA Modules:
  0.0 66.6 jit_solution(15679333815919232538)
XLA Ops:
  0.6 65.0 %shard_map.41 = (f32[256,512]{1,0:T(8,128)S(1)}, f32[256,512]{1,0:T(8,128)S(1)}) custom-call(f32[256,4096]{1,0:T(8,128)} %first.1, f32[256,4096]{1,0:T(8,128)} %second.1), custom_call_target="tpu_custom_call" | custom-call | tf_op jit(solution)/shard_map/pallas_call | solution.py:592
  65.6 1.0 %shard_map.42 = (f32[256,512]{1,0:T(8,128)}, f32[256,512]{1,0:T(8,128)}) custom-call(f32[256,512]{1,0:T(8,128)S(1)} %get-tuple-element.4.a, f32[256,512]{1,0:T(8,128)S(1)} %get-tuple-element.5.b), custom_call_target="tpu_custom_call" | custom-call | tf_op jit(solution)/shard_map/pallas_call | solution.py:647

commit v13 on v12

--- a/solution.py
+++ b/solution.py
@@ -471,9 +471,10 @@
         return [a, send(m + 5, p1.at[ph, 2, low], p1in.at[ph, 0, low], sib)]
 
     lax.fori_loop(2, 4, step, 0)
-    lax.fori_loop(0, 2, lambda n, carry: (uses(3, n), carry)[1], 0)
+    uses(3, 0)
+    arrive(4, True, None)
+    uses(3, 1)
     relay1, in1 = p1_start(0, iz)
-    arrive(4, True, None)
     from_core(4, 0, 0)
     from_core(4, 1, 1)
     use(lax.rem(z + 4, 8))
@@ -534,18 +535,18 @@
     in2 = p2_send(1)
     relay1, more = p1_start(1, 1 - iz)
     in1 += more
+    in2 += p2_add(1, relay2)
     relay20 = p2_relay(0)
-    in2 += p2_add(1, relay2)
     in20 = p2_send(0)
     ob2[0] = partial2(0, 1)
     ob2[1] = partial2(0, 0)
     in1 += p1_add(1, relay1)
     in20 += p2_add(0, relay20)
-    finish_sends()
     for cp in in2:
         cp.wait_recv()
     xs[...] = (ob2[0] + p2in[0, 1].astype(F32) + p2in[1, 1].astype(F32)).astype(BF16)
     x_last = send(M_X, xs, xr, sib)
+    finish_sends()
     ob1[0] = partial1(iz, 0)
     ob1[1] = partial1(1 - iz, 0)
     outs = []

time: 67 us -> 66.9 us (level)
  no operation moved by 1% of the time
where the time goes in v13:
time: 66.9 us; the launch traced here: 66.4 us
  Pallas kernels  65.8 us (98%)
    pallas_call x1, Pallas kernels, body(): pl.pallas_call(kernel, out_shape=(out, out), in_specs=[anywhere, anywhere...  64.8 us

profile of v13, /device:TPU:1, one launch (start us, length us, event | category | flops | bytes accessed | tf_op | source)
XLA Modules:
  0.0 66.4 jit_solution(15721793322257498713)
XLA Ops:
  0.6 64.8 %shard_map.41 = (f32[256,512]{1,0:T(8,128)S(1)}, f32[256,512]{1,0:T(8,128)S(1)}) custom-call(f32[256,4096]{1,0:T(8,128)} %first.1, f32[256,4096]{1,0:T(8,128)} %second.1), custom_call_target="tpu_custom_call" | custom-call | tf_op jit(solution)/shard_map/pallas_call | solution.py:593
  65.4 1.0 %shard_map.42 = (f32[256,512]{1,0:T(8,128)}, f32[256,512]{1,0:T(8,128)}) custom-call(f32[256,512]{1,0:T(8,128)S(1)} %get-tuple-element.4.a, f32[256,512]{1,0:T(8,128)S(1)} %get-tuple-element.5.b), custom_call_target="tpu_custom_call" | custom-call | tf_op jit(solution)/shard_map/pallas_call | solution.py:648

commit v14 on v13

--- a/solution.py
+++ b/solution.py
@@ -399,42 +399,46 @@
                     both = g.at[c, source, pl.ds(2 * u, 2)]
                     make(M_GD + 4 * t + 2 * d + u, both, both, core).start()
 
-    def use(zs_):
+    def use(zs_, o):
+        rows = pl.ds(256 * o, 256)
         i = lax.div(zs_, 4)
         k = lax.rem(zs_, 4)
         ga = jnp.concatenate([g[0, zs_].reshape(256, 256), g[1, zs_].reshape(256, 256)], 0)
-        v = nt(nrm[kb(k)], ga)
-        acc1[i] += v[:, 0:256]
-        acc1[2 + i] += v[:, 256:512]
-        acc2[k] += nn(jnp.concatenate([nrm[i], nrm[4 + i]], 1), ga)
-        v = ga.astype(F32)
-        s = v * v
-        part = s[:, 0:128] + s[:, 128:256]
-        rsq[i] += part[0:256]
-        rsq[2 + i] += part[256:512]
-        csq[k] += jnp.sum(s.reshape(64, 8, 256), 0)
+        v = nt(nrm[kb(k), rows], ga)
+        acc1[i, rows] += v[:, 0:256]
+        acc1[2 + i, rows] += v[:, 256:512]
+        acc2[k, rows] += nn(jnp.concatenate([nrm[i, rows], nrm[4 + i, rows]], 1), ga)
+        if o == 0:
+            v = ga.astype(F32)
+            s = v * v
+            part = s[:, 0:128] + s[:, 128:256]
+            rsq[i] += part[0:256]
+            rsq[2 + i] += part[256:512]
+            csq[k] += jnp.sum(s.reshape(64, 8, 256), 0)
 
     def from_core(t, d, u):
         part = g.at[0, 0, pl.ds(0, 2)]
         make(M_GD + 4 * t + 2 * d + u, part, part, core).wait_recv()
 
-    def uses(t, n):
+    def uses(t, n, halves):
         for u in range(2):
             from_core(t, n, u)
-        use(lax.rem(z + (8 - t) + n * 2 * t, 8))
+        for o in halves:
+            use(lax.rem(z + (8 - t) + n * 2 * t, 8), o)
 
     arrive(1, True, True)
     arrive(1, False, True)
-    for cp in x_in[2:] + x_ring[2:]:
-        cp.wait_recv()
-    norms(1)
-    uses(0, 0)
+    uses(0, 0, (0,))
 
     def step(t, carry):
         arrive(t, True, True)
-        uses(t - 1, 0)
+        uses(t - 1, 0, (0,))
         arrive(t, False, t < 3)
-        uses(t - 1, 1)
+        uses(t - 1, 1, (0,))
+        return carry
+
+    def rest(n, carry):
+        use(lax.rem(z + 6 + n, 8), 1)
         return carry
 
     def partial1(a, o):
@@ -471,13 +475,18 @@
         return [a, send(m + 5, p1.at[ph, 2, low], p1in.at[ph, 0, low], sib)]
 
     lax.fori_loop(2, 4, step, 0)
-    uses(3, 0)
+    for cp in x_in[2:] + x_ring[2:]:
+        cp.wait_recv()
+    norms(1)
+    lax.fori_loop(0, 5, rest, 0)
     arrive(4, True, None)
-    uses(3, 1)
+    uses(3, 0, (0, 1))
+    uses(3, 1, (0, 1))
     relay1, in1 = p1_start(0, iz)
     from_core(4, 0, 0)
     from_core(4, 1, 1)
-    use(lax.rem(z + 4, 8))
+    use(lax.rem(z + 4, 8), 1)
+    use(lax.rem(z + 4, 8), 0)
 
     for k in range(4):
         colsq[k] = jnp.sum(csq[k], 0, keepdims=True) * (0.5 / LAMBDA)

time: 66.9 us -> 67 us (level); the launches traced: 66.4 us -> 65.8 us
  no operation moved by 1% of the time
where the time goes in v14:
time: 67 us; the launch traced here: 65.8 us
  Pallas kernels  65.2 us (97%)
    pallas_call x1, Pallas kernels, body(): pl.pallas_call(kernel, out_shape=(out, out), in_specs=[anywhere, anywhere...  64.2 us

profile of v14, /device:TPU:1, one launch (start us, length us, event | category | flops | bytes accessed | tf_op | source)
XLA Modules:
  0.0 65.8 jit_solution(189049155679552093)
XLA Ops:
  0.6 64.2 %shard_map.41 = (f32[256,512]{1,0:T(8,128)S(1)}, f32[256,512]{1,0:T(8,128)S(1)}) custom-call(f32[256,4096]{1,0:T(8,128)} %first.1, f32[256,4096]{1,0:T(8,128)} %second.1), custom_call_target="tpu_custom_call" | custom-call | tf_op jit(solution)/shard_map/pallas_call | solution.py:602
  64.8 1.0 %shard_map.42 = (f32[256,512]{1,0:T(8,128)}, f32[256,512]{1,0:T(8,128)}) custom-call(f32[256,512]{1,0:T(8,128)S(1)} %get-tuple-element.4.a, f32[256,512]{1,0:T(8,128)S(1)} %get-tuple-element.5.b), custom_call_target="tpu_custom_call" | custom-call | tf_op jit(solution)/shard_map/pallas_call | solution.py:657
